TPU v7x, 256 devices: a whole 4x4x8 slice. The times are simulated.
256 devices in a mesh: segment: 8 (over y, x_hi), dp: 32 (over z, x_lo, core).
Axes of the slice: x: 4 (x_hi: 2, x_lo: 2; x = x_hi * 2 + x_lo), y: 4, z: 8, core: 2. Of those that a mesh axis runs over, the one named last changes fastest.
Arguments:
- features: bfloat16 [128, 144, 512], P('dp'), may hold values from -6 to 6
- labels: int32 [128], P('dp'), may hold values from 0 to 3
- classifier: float32 [512, 4], replicated, may hold values from -1.5 to 1.5
- w_mix: bfloat16 [24, 512, 512], P('segment'), may hold values from -0.25 to 0.25
- w_point: bfloat16 [24, 512, 512], P('segment'), may hold values from -0.25 to 0.25
- kernels: bfloat16 [24, 9, 512], P('segment'), may hold values from -2 to 2
- counts: int32 [8], P('segment'), may hold values from 1 to 3, 20 in all
Outputs:
- grad_mix: float32 [24, 512, 512], P('segment')
- grad_point: float32 [24, 512, 512], P('segment')
- grad_kernel: float32 [24, 9, 512], P('segment')
Inputs may be any that keep to these rules, and one draw needn't show every extreme that they name: Section s holds counts[s] cells; together 20, the largest 3.
All inputs are finite; a program needn't handle non-finite values. No bound on the sum of `counts` on one device may be relied on, other than what follows from the above.
Results may differ from a plain program's by a relative error of at most 0.012.
Values may be sent and summed in bfloat16 or wider, within the bound.
A program may use at most 128 MiB of HBM per device.

v0:
```python
import jax
import jax.numpy as jnp
from jax import lax
from jax.sharding import PartitionSpec as P

GRID = 12


EPSILON = 1e-06


def shifted(value, axis, by):
    length = lax.axis_size(axis)
    pairs = [(i, i + by) for i in range(length) if 0 <= i + by < length]
    return lax.ppermute(value, axis, pairs)


def depthwise(rectified, kernel_row, grid_side):
    shape_in = rectified.shape
    image = rectified.astype(jnp.float32).reshape(
        shape_in[:-2] + (grid_side, grid_side, shape_in[-1])
    )
    padded = jnp.pad(image, [(0, 0)] * (image.ndim - 3) + [(1, 1), (1, 1), (0, 0)])
    taps = kernel_row.astype(jnp.float32)
    total = jnp.zeros(image.shape, jnp.float32)
    for row_off in range(3):
        for col_off in range(3):
            total = (
                total
                + taps[3 * row_off + col_off]
                * padded[..., row_off : row_off + grid_side, col_off : col_off + grid_side, :]
            )
    return total.reshape(shape_in)


def depthwise_back(rectified, kernel_row, upstream, grid_side):
    shape_in = rectified.shape
    image = rectified.astype(jnp.float32).reshape(
        shape_in[:-2] + (grid_side, grid_side, shape_in[-1])
    )
    padding = [(0, 0)] * (image.ndim - 3) + [(1, 1), (1, 1), (0, 0)]
    padded_in = jnp.pad(image, padding)
    upstream_img = upstream.reshape(image.shape)
    padded_up = jnp.pad(upstream_img, padding)
    taps = kernel_row.astype(jnp.float32)
    summed_axes = tuple(range(image.ndim - 1))
    tap_grads = []
    input_grad = jnp.zeros(image.shape, jnp.float32)
    for row_off in range(3):
        for col_off in range(3):
            window = padded_in[..., row_off : row_off + grid_side, col_off : col_off + grid_side, :]
            tap_grads.append(jnp.sum(window * upstream_img, axis=summed_axes))
            moved = padded_up[
                ..., 2 - row_off : 2 - row_off + grid_side, 2 - col_off : 2 - col_off + grid_side, :
            ]
            input_grad = input_grad + taps[3 * row_off + col_off] * moved
    return (jnp.stack(tap_grads), input_grad.reshape(shape_in))


def cell_forward(prev_act, older_act, mix_weight, point_weight, kernel_row, grid_side):
    rect_prev = jax.nn.relu(prev_act)
    rect_older = jax.nn.relu(older_act)
    separable = depthwise(rect_older, kernel_row, grid_side).astype(jnp.bfloat16)
    branches = jnp.dot(separable, point_weight, preferred_element_type=jnp.float32)
    branches = branches + jnp.dot(rect_prev, mix_weight, preferred_element_type=jnp.float32)
    summed = prev_act.astype(jnp.float32) + branches
    scale = lax.rsqrt(jnp.mean(summed * summed, axis=-1, keepdims=True) + EPSILON)
    return ((summed * scale).astype(jnp.bfloat16), separable, summed)


def cell_backward(
    prev_act,
    older_act,
    separable,
    summed,
    mix_weight,
    point_weight,
    kernel_row,
    grad_new,
    grad_pass,
    grid_side,
):
    scale = lax.rsqrt(jnp.mean(summed * summed, axis=-1, keepdims=True) + EPSILON)
    normed = summed * scale
    grad_norm = grad_new.astype(jnp.float32)
    grad_sum = scale * (grad_norm - normed * jnp.mean(grad_norm * normed, axis=-1, keepdims=True))
    grad_half = grad_sum.astype(jnp.bfloat16)
    point_grad = jnp.dot(separable.T, grad_half, preferred_element_type=jnp.float32)
    mix_grad = jnp.dot(jax.nn.relu(prev_act).T, grad_half, preferred_element_type=jnp.float32)
    sep_grad = jnp.dot(grad_half, point_weight.T, preferred_element_type=jnp.float32)
    prev_mix = jnp.dot(grad_half, mix_weight.T, preferred_element_type=jnp.float32)
    grad_prev = (
        grad_sum + jnp.where(prev_act > 0, prev_mix, 0.0) + grad_pass.astype(jnp.float32)
    ).astype(jnp.bfloat16)
    kernel_grad, older_rect = depthwise_back(
        jax.nn.relu(older_act), kernel_row, sep_grad, grid_side
    )
    grad_older = jnp.where(older_act > 0, older_rect, 0.0).astype(jnp.bfloat16)
    return (grad_prev, grad_older, mix_grad, point_grad, kernel_grad)


def head_grad(final_act, image_labels, classifier):
    pooled = jnp.mean(jax.nn.relu(final_act).astype(jnp.float32), axis=-2)
    logits = jnp.dot(pooled, classifier, precision=lax.Precision.HIGHEST)
    classes = jnp.arange(classifier.shape[1], dtype=jnp.int32)
    onehot = (image_labels[..., None] == classes).astype(jnp.float32)
    grad_pool = jnp.dot(logits - onehot, classifier.T, precision=lax.Precision.HIGHEST)
    return jnp.where(final_act > 0, grad_pool[..., None, :] / final_act.shape[-2], 0.0).astype(
        jnp.bfloat16
    )


def shards(features, labels, classifier, w_mix, w_point, kernels, counts):
    micro, pixels, channels = features.shape
    slots = w_mix.shape[0]
    segments = lax.axis_size("segment")
    position = lax.axis_index("segment")
    slot_count = counts[0]
    last_segment = segments - 1
    tick_total = micro + segments - 1
    blank_act = jnp.zeros((pixels, channels), jnp.bfloat16)
    blank_sum = jnp.zeros((pixels, channels), jnp.float32)

    def run_section(prev_act, older_act):
        records = []
        for slot in range(slots):

            def active_cell(prev_act=prev_act, older_act=older_act, slot=slot):
                new_act, separable, summed = cell_forward(
                    prev_act, older_act, w_mix[slot], w_point[slot], kernels[slot], GRID
                )
                return (new_act, prev_act, separable, summed)

            def run_skipped(prev_act=prev_act, older_act=older_act):
                return (prev_act, older_act, blank_act, blank_sum)

            new_act, new_older, separable, summed = lax.cond(
                slot < slot_count, active_cell, run_skipped
            )
            records.append((prev_act, older_act, separable, summed))
            prev_act, older_act = (new_act, new_older)
        return (prev_act, older_act, records)

    store = (
        jnp.zeros((micro, slots, 2, pixels, channels), jnp.bfloat16),
        jnp.zeros((micro, slots, pixels, channels), jnp.bfloat16),
        jnp.zeros((micro, slots, pixels, channels), jnp.float32),
    )

    def save(store, batch_pos, records):
        pairs = jnp.stack([jnp.stack([entry[0], entry[1]]) for entry in records])
        seps = jnp.stack([entry[2] for entry in records])
        sums = jnp.stack([entry[3] for entry in records])
        result = (
            lax.dynamic_update_index_in_dim(store[0], pairs, batch_pos, 0),
            lax.dynamic_update_index_in_dim(store[1], seps, batch_pos, 0),
            lax.dynamic_update_index_in_dim(store[2], sums, batch_pos, 0),
        )
        return result

    def load(store, batch_pos):
        pairs = lax.dynamic_index_in_dim(store[0], batch_pos, 0, keepdims=False)
        seps = lax.dynamic_index_in_dim(store[1], batch_pos, 0, keepdims=False)
        sums = lax.dynamic_index_in_dim(store[2], batch_pos, 0, keepdims=False)
        records = [
            (pairs[slot, 0], pairs[slot, 1], seps[slot], sums[slot]) for slot in range(slots)
        ]
        return records

    finals = jnp.zeros((micro, pixels, channels), jnp.bfloat16)

    def forward_tick(tick, carry):
        recv_prev, recv_older, store, finals = carry
        batch_raw = tick - position
        valid = (batch_raw >= 0) & (batch_raw < micro)
        batch_pos = jnp.clip(batch_raw, 0, micro - 1)
        entry = lax.dynamic_index_in_dim(features, batch_pos, 0, keepdims=False)
        prev_act = jnp.where(position == 0, entry, recv_prev)
        older_act = jnp.where(position == 0, entry, recv_older)

        def forward_work():
            out_prev, out_older, records = run_section(prev_act, older_act)
            new_store = save(store, batch_pos, records)
            label_now = lax.dynamic_slice_in_dim(labels, batch_pos, 1)
            start_grad = lax.cond(
                position == last_segment,
                lambda: head_grad(out_prev[None], label_now, classifier)[0],
                lambda: blank_act,
            )
            new_finals = lax.dynamic_update_index_in_dim(finals, start_grad, batch_pos, 0)
            return (out_prev, out_older, new_store, new_finals)

        def forward_resting():
            return (prev_act, older_act, store, finals)

        out_prev, out_older, store, finals = lax.cond(valid, forward_work, forward_resting)
        arrived = shifted(jnp.stack([out_prev, out_older]), "segment", 1)
        return (arrived[0], arrived[1], store, finals)

    carry = lax.fori_loop(0, tick_total, forward_tick, (blank_act, blank_act, store, finals))
    store = carry[2]
    finals = carry[3]
    grads_zero = (
        jnp.zeros((slots, channels, channels), jnp.float32),
        jnp.zeros((slots, channels, channels), jnp.float32),
        jnp.zeros((slots, 9, channels), jnp.float32),
    )

    def backward_tick(tick, carry):
        recv_prev, recv_older, grads = carry
        batch_raw = tick - (last_segment - position)
        valid = (batch_raw >= 0) & (batch_raw < micro)
        batch_pos = jnp.clip(batch_raw, 0, micro - 1)
        own_grad = lax.dynamic_index_in_dim(finals, batch_pos, 0, keepdims=False)
        grad_prev = jnp.where(position == last_segment, own_grad, recv_prev)
        grad_older = jnp.where(position == last_segment, blank_act, recv_older)

        def backward_work():
            records = load(store, batch_pos)
            grad_front, grad_back, accum = (grad_prev, grad_older, grads)
            for slot in reversed(range(slots)):

                def active_back(grad_front=grad_front, grad_back=grad_back, accum=accum, slot=slot):
                    prev_act, older_act, separable, summed = records[slot]
                    new_front, new_back, mix_grad, point_grad, kernel_grad = cell_backward(
                        prev_act,
                        older_act,
                        separable,
                        summed,
                        w_mix[slot],
                        w_point[slot],
                        kernels[slot],
                        grad_front,
                        grad_back,
                        GRID,
                    )
                    return (
                        new_front,
                        new_back,
                        (
                            accum[0].at[slot].add(mix_grad),
                            accum[1].at[slot].add(point_grad),
                            accum[2].at[slot].add(kernel_grad),
                        ),
                    )

                def work_skipped(grad_front=grad_front, grad_back=grad_back, accum=accum):
                    return (grad_front, grad_back, accum)

                grad_front, grad_back, accum = lax.cond(
                    slot < slot_count, active_back, work_skipped
                )
            return (grad_front, grad_back, accum)

        def backward_resting():
            return (grad_prev, grad_older, grads)

        grad_prev, grad_older, grads = lax.cond(valid, backward_work, backward_resting)
        arrived = shifted(jnp.stack([grad_prev, grad_older]), "segment", -1)
        return (arrived[0], arrived[1], grads)

    carry = lax.fori_loop(0, tick_total, backward_tick, (blank_act, blank_act, grads_zero))
    totals = lax.psum(carry[2], "dp")
    return (totals[0], totals[1], totals[2])


def solution(mesh):
    return jax.shard_map(
        shards,
        mesh=mesh,
        in_specs=(
            P("dp", None, None),
            P("dp"),
            P(),
            P("segment", None, None),
            P("segment", None, None),
            P("segment", None, None),
            P("segment"),
        ),
        out_specs=(P("segment", None, None), P("segment", None, None), P("segment", None, None)),
        check_vma=False,
    )
```

profile of v0, /device:TPU:1, one launch (start us, length us, event | category | flops | bytes accessed | tf_op | source)
XLA Modules:
  0.0 1710.5 jit_solution(17687244346941689218)
XLA Ops:
  15.9 320.7 %while.56 = (s32[]{:T(128)}, bf16[144,512]{1,0:T(8,128)(2,1)}, bf16[144,512]{1,0:T(8,128)(2,1)}, bf16[4,3,2,144,512]{4,3,2,1,0:T(8,128)(2,1)}, bf16[4,3,144,512]...) while((s32[]{:T(128)}, bf16[144,512]{1,0:T(8,128)(2,1)}, ...), condition=%wide.region_15.16_spmd, body=%wide.region_0.15_spmd.sunk | while | flops 464919488 | bytes 27028164 | solution.py:200
  19.4 22.5 %conditional.11 = (bf16[4,3,2,144,512]{4,3,2,1,0:T(8,128)(2,1)}, bf16[4,3,144,512]{3,2,1,0:T(8,128)(2,1)}, f32[4,3,144,512]{3,2,1,0:T(8,128)}, bf16[4,144,512]{2...) conditional(s32[]{:T(128)} %convert_element_type.274, ...), branch_computations={%region_1.1_spmd, %region_2.14_spmd} | conditional | flops 464624576 | bytes 23341316 | solution.py:196
  52.1 22.6 %conditional.11 = (bf16[4,3,2,144,512]{4,3,2,1,0:T(8,128)(2,1)}, bf16[4,3,144,512]{3,2,1,0:T(8,128)(2,1)}, f32[4,3,144,512]{3,2,1,0:T(8,128)}, bf16[4,144,512]{2...) conditional(s32[]{:T(128)} %convert_element_type.274, ...), branch_computations={%region_1.1_spmd, %region_2.14_spmd} | conditional | flops 464624576 | bytes 23341316 | solution.py:196
  89.0 22.5 %conditional.11 = (bf16[4,3,2,144,512]{4,3,2,1,0:T(8,128)(2,1)}, bf16[4,3,144,512]{3,2,1,0:T(8,128)(2,1)}, f32[4,3,144,512]{3,2,1,0:T(8,128)}, bf16[4,144,512]{2...) conditional(s32[]{:T(128)} %convert_element_type.274, ...), branch_computations={%region_1.1_spmd, %region_2.14_spmd} | conditional | flops 464624576 | bytes 23341316 | solution.py:196
  125.9 22.5 %conditional.11 = (bf16[4,3,2,144,512]{4,3,2,1,0:T(8,128)(2,1)}, bf16[4,3,144,512]{3,2,1,0:T(8,128)(2,1)}, f32[4,3,144,512]{3,2,1,0:T(8,128)}, bf16[4,144,512]{2...) conditional(s32[]{:T(128)} %convert_element_type.274, ...), branch_computations={%region_1.1_spmd, %region_2.14_spmd} | conditional | flops 464624576 | bytes 23341316 | solution.py:196
  163.8 28.0 %collective-permute-start = (bf16[2,144,512]{2,1,0:T(8,128)(2,1)S(1)}, bf16[2,144,512]{2,1,0:T(8,128)(2,1)S(1)}, u32[]{:S(2)}, u32[]{:S(2)}) collective-permute-start(bf16[2,144,512]{2,1,0:T(8,128)(2,1)S(1)} %pad_maximum_fusion.4), channel_id=1, source_target_pairs={{0,32},{32,64},{64,96},{96,128},{128,160},{160,192},{192,224},{1,3... | collective-permute-start | bytes 884744 | tf_op jit(solution)/shard_map/while/body/eval_jaxpr/ppermute | solution.py:15
  215.0 28.2 %collective-permute-start = (bf16[2,144,512]{2,1,0:T(8,128)(2,1)S(1)}, bf16[2,144,512]{2,1,0:T(8,128)(2,1)S(1)}, u32[]{:S(2)}, u32[]{:S(2)}) collective-permute-start(bf16[2,144,512]{2,1,0:T(8,128)(2,1)S(1)} %pad_maximum_fusion.4), channel_id=1, source_target_pairs={{0,32},{32,64},{64,96},{96,128},{128,160},{160,192},{192,224},{1,3... | collective-permute-start | bytes 884744 | tf_op jit(solution)/shard_map/while/body/eval_jaxpr/ppermute | solution.py:15
  267.3 23.7 %collective-permute-start = (bf16[2,144,512]{2,1,0:T(8,128)(2,1)S(1)}, bf16[2,144,512]{2,1,0:T(8,128)(2,1)S(1)}, u32[]{:S(2)}, u32[]{:S(2)}) collective-permute-start(bf16[2,144,512]{2,1,0:T(8,128)(2,1)S(1)} %pad_maximum_fusion.4), channel_id=1, source_target_pairs={{0,32},{32,64},{64,96},{96,128},{128,160},{160,192},{192,224},{1,3... | collective-permute-start | bytes 884744 | tf_op jit(solution)/shard_map/while/body/eval_jaxpr/ppermute | solution.py:15
  315.1 17.2 %collective-permute-start = (bf16[2,144,512]{2,1,0:T(8,128)(2,1)S(1)}, bf16[2,144,512]{2,1,0:T(8,128)(2,1)S(1)}, u32[]{:S(2)}, u32[]{:S(2)}) collective-permute-start(bf16[2,144,512]{2,1,0:T(8,128)(2,1)S(1)} %pad_maximum_fusion.4), channel_id=1, source_target_pairs={{0,32},{32,64},{64,96},{96,128},{128,160},{160,192},{192,224},{1,3... | collective-permute-start | bytes 884744 | tf_op jit(solution)/shard_map/while/body/eval_jaxpr/ppermute | solution.py:15
  341.1 1080.0 %while.57 = (s32[]{:T(128)}, bf16[144,512]{1,0:T(8,128)(2,1)}, bf16[144,512]{1,0:T(8,128)(2,1)}, f32[3,512,512]{2,1,0:T(8,128)S(1)}, f32[3,512,512]{1,2,0:T(8,12...) while((s32[]{:T(128)}, bf16[144,512]{1,0:T(8,128)(2,1)}, ...), condition=%wide.region_58.59_spmd, body=%wide.region_16.58_spmd.sunk | while | flops 922449792 | bytes 125047040 | solution.py:262
  362.9 26.8 %collective-permute-done.1 = bf16[2,144,512]{2,1,0:T(8,128)(2,1)S(1)} collective-permute-done((bf16[2,144,512]{2,1,0:T(8,128)(2,1)}, bf16[2,144,512]{2,1,0:T(8,128)(2,1)S(1)}, u32[]{:S(2)}, u32[]{:S(2)}) %collective-permute-start.1) | collective-permute-done | bytes 294944 | tf_op jit(solution)/shard_map/while/body/eval_jaxpr/ppermute | solution.py:15
  437.8 20.4 %collective-permute-done.1 = bf16[2,144,512]{2,1,0:T(8,128)(2,1)S(1)} collective-permute-done((bf16[2,144,512]{2,1,0:T(8,128)(2,1)}, bf16[2,144,512]{2,1,0:T(8,128)(2,1)S(1)}, u32[]{:S(2)}, u32[]{:S(2)}) %collective-permute-start.1) | collective-permute-done | bytes 294944 | tf_op jit(solution)/shard_map/while/body/eval_jaxpr/ppermute | solution.py:15
  463.6 17.2 %collective-permute-done.1 = bf16[2,144,512]{2,1,0:T(8,128)(2,1)S(1)} collective-permute-done((bf16[2,144,512]{2,1,0:T(8,128)(2,1)}, bf16[2,144,512]{2,1,0:T(8,128)(2,1)S(1)}, u32[]{:S(2)}, u32[]{:S(2)}) %collective-permute-start.1) | collective-permute-done | bytes 294944 | tf_op jit(solution)/shard_map/while/body/eval_jaxpr/ppermute | solution.py:15
  486.2 528.6 %collective-permute-done.1 = bf16[2,144,512]{2,1,0:T(8,128)(2,1)S(1)} collective-permute-done((bf16[2,144,512]{2,1,0:T(8,128)(2,1)}, bf16[2,144,512]{2,1,0:T(8,128)(2,1)S(1)}, u32[]{:S(2)}, u32[]{:S(2)}) %collective-permute-start.1) | collective-permute-done | bytes 294944 | tf_op jit(solution)/shard_map/while/body/eval_jaxpr/ppermute | solution.py:15
  1017.3 87.4 %conditional.12 = ((f32[3,512,512]{2,1,0:T(8,128)S(1)}, f32[3,512,512]{1,2,0:T(8,128)}, f32[3,9,512]{2,1,0:T(8,128)}, bf16[1,144,512]{2,1,0:T(8,128)(2,1)S(1)}, bf16[1,144,512]{2,1,0:T(8,128)(2,1)})) conditional(s32[]{:T(128)} %convert_element_type.275, (bf16[144,512]{1,0:T(8,128)(2,1)S(1)}, bf16[144,512]{1,0:T(8,128)(2,1)}, ...), branch_computations={%region_17.17_spmd, %region_18.57_spmd} | conditional | flops 922154880 | bytes 121950032 | solution.py:258
  1024.2 23.8 %conditional.5 = (bf16[144,512]{1,0:T(8,128)(2,1)S(1)}, bf16[144,512]{1,0:T(8,128)(2,1)}, f32[3,512,512]{2,1,0:T(8,128)S(1)}, f32[3,512,512]{1,2,0:T(8,128)}, f32[3,9,512]{2,1,0:T(8,128)}) conditional(s32[]{:T(128)} %convert_element_type.202, (bf16[144,512]{1,0:T(8,128)(2,1)S(1)}, bf16[144,512]{1,0:T(8,128)(2,1)}, f32[3,512,512]{2,1,0:T(8,128)S(1)}, ...), branch_computations={%region_19.18_spmd, %region_20.30_spmd} | conditional | flops 307384960 | bytes 38799412 | solution.py:250
  1048.7 23.7 %conditional.6 = (bf16[144,512]{1,0:T(8,128)(2,1)S(1)}, bf16[144,512]{1,0:T(8,128)(2,1)}, f32[3,512,512]{2,1,0:T(8,128)S(1)}, f32[3,512,512]{1,2,0:T(8,128)}, f32[3,9,512]{2,1,0:T(8,128)}) conditional(s32[]{:T(128)} %convert_element_type.201, (bf16[144,512]{1,0:T(8,128)(2,1)S(1)}, bf16[144,512]{1,0:T(8,128)(2,1)}, f32[3,512,512]{2,1,0:T(8,128)S(1)}, ...), branch_computations={%region_32.31_spmd, %region_33.43_spmd} | conditional | flops 307384960 | bytes 38799412 | solution.py:250
  1077.0 27.6 %conditional.7 = (f32[3,512,512]{2,1,0:T(8,128)S(1)}, f32[3,512,512]{1,2,0:T(8,128)}, f32[3,9,512]{2,1,0:T(8,128)}, bf16[1,144,512]{2,1,0:T(8,128)(2,1)S(1)}, bf16[1,144,512]{2,1,0:T(8,128)(2,1)}) conditional(s32[]{:T(128)} %convert_element_type.200, (bf16[144,512]{1,0:T(8,128)(2,1)S(1)}, bf16[144,512]{1,0:T(8,128)(2,1)}, ...), branch_computations={%region_45.44_spmd, %region_46.56_spmd} | conditional | flops 307384960 | bytes 36977952 | solution.py:250
  1118.9 87.4 %conditional.12 = ((f32[3,512,512]{2,1,0:T(8,128)S(1)}, f32[3,512,512]{1,2,0:T(8,128)}, f32[3,9,512]{2,1,0:T(8,128)}, bf16[1,144,512]{2,1,0:T(8,128)(2,1)S(1)}, bf16[1,144,512]{2,1,0:T(8,128)(2,1)})) conditional(s32[]{:T(128)} %convert_element_type.275, (bf16[144,512]{1,0:T(8,128)(2,1)S(1)}, bf16[144,512]{1,0:T(8,128)(2,1)}, ...), branch_computations={%region_17.17_spmd, %region_18.57_spmd} | conditional | flops 922154880 | bytes 121950032 | solution.py:258
  1125.8 23.8 %conditional.5 = (bf16[144,512]{1,0:T(8,128)(2,1)S(1)}, bf16[144,512]{1,0:T(8,128)(2,1)}, f32[3,512,512]{2,1,0:T(8,128)S(1)}, f32[3,512,512]{1,2,0:T(8,128)}, f32[3,9,512]{2,1,0:T(8,128)}) conditional(s32[]{:T(128)} %convert_element_type.202, (bf16[144,512]{1,0:T(8,128)(2,1)S(1)}, bf16[144,512]{1,0:T(8,128)(2,1)}, f32[3,512,512]{2,1,0:T(8,128)S(1)}, ...), branch_computations={%region_19.18_spmd, %region_20.30_spmd} | conditional | flops 307384960 | bytes 38799412 | solution.py:250
  1150.3 23.7 %conditional.6 = (bf16[144,512]{1,0:T(8,128)(2,1)S(1)}, bf16[144,512]{1,0:T(8,128)(2,1)}, f32[3,512,512]{2,1,0:T(8,128)S(1)}, f32[3,512,512]{1,2,0:T(8,128)}, f32[3,9,512]{2,1,0:T(8,128)}) conditional(s32[]{:T(128)} %convert_element_type.201, (bf16[144,512]{1,0:T(8,128)(2,1)S(1)}, bf16[144,512]{1,0:T(8,128)(2,1)}, f32[3,512,512]{2,1,0:T(8,128)S(1)}, ...), branch_computations={%region_32.31_spmd, %region_33.43_spmd} | conditional | flops 307384960 | bytes 38799412 | solution.py:250
  1178.6 27.6 %conditional.7 = (f32[3,512,512]{2,1,0:T(8,128)S(1)}, f32[3,512,512]{1,2,0:T(8,128)}, f32[3,9,512]{2,1,0:T(8,128)}, bf16[1,144,512]{2,1,0:T(8,128)(2,1)S(1)}, bf16[1,144,512]{2,1,0:T(8,128)(2,1)}) conditional(s32[]{:T(128)} %convert_element_type.200, (bf16[144,512]{1,0:T(8,128)(2,1)S(1)}, bf16[144,512]{1,0:T(8,128)(2,1)}, ...), branch_computations={%region_45.44_spmd, %region_46.56_spmd} | conditional | flops 307384960 | bytes 36977952 | solution.py:250
  1220.5 87.4 %conditional.12 = ((f32[3,512,512]{2,1,0:T(8,128)S(1)}, f32[3,512,512]{1,2,0:T(8,128)}, f32[3,9,512]{2,1,0:T(8,128)}, bf16[1,144,512]{2,1,0:T(8,128)(2,1)S(1)}, bf16[1,144,512]{2,1,0:T(8,128)(2,1)})) conditional(s32[]{:T(128)} %convert_element_type.275, (bf16[144,512]{1,0:T(8,128)(2,1)S(1)}, bf16[144,512]{1,0:T(8,128)(2,1)}, ...), branch_computations={%region_17.17_spmd, %region_18.57_spmd} | conditional | flops 922154880 | bytes 121950032 | solution.py:258
  1227.4 23.8 %conditional.5 = (bf16[144,512]{1,0:T(8,128)(2,1)S(1)}, bf16[144,512]{1,0:T(8,128)(2,1)}, f32[3,512,512]{2,1,0:T(8,128)S(1)}, f32[3,512,512]{1,2,0:T(8,128)}, f32[3,9,512]{2,1,0:T(8,128)}) conditional(s32[]{:T(128)} %convert_element_type.202, (bf16[144,512]{1,0:T(8,128)(2,1)S(1)}, bf16[144,512]{1,0:T(8,128)(2,1)}, f32[3,512,512]{2,1,0:T(8,128)S(1)}, ...), branch_computations={%region_19.18_spmd, %region_20.30_spmd} | conditional | flops 307384960 | bytes 38799412 | solution.py:250
  1251.9 23.7 %conditional.6 = (bf16[144,512]{1,0:T(8,128)(2,1)S(1)}, bf16[144,512]{1,0:T(8,128)(2,1)}, f32[3,512,512]{2,1,0:T(8,128)S(1)}, f32[3,512,512]{1,2,0:T(8,128)}, f32[3,9,512]{2,1,0:T(8,128)}) conditional(s32[]{:T(128)} %convert_element_type.201, (bf16[144,512]{1,0:T(8,128)(2,1)S(1)}, bf16[144,512]{1,0:T(8,128)(2,1)}, f32[3,512,512]{2,1,0:T(8,128)S(1)}, ...), branch_computations={%region_32.31_spmd, %region_33.43_spmd} | conditional | flops 307384960 | bytes 38799412 | solution.py:250
  1280.2 27.6 %conditional.7 = (f32[3,512,512]{2,1,0:T(8,128)S(1)}, f32[3,512,512]{1,2,0:T(8,128)}, f32[3,9,512]{2,1,0:T(8,128)}, bf16[1,144,512]{2,1,0:T(8,128)(2,1)S(1)}, bf16[1,144,512]{2,1,0:T(8,128)(2,1)}) conditional(s32[]{:T(128)} %convert_element_type.200, (bf16[144,512]{1,0:T(8,128)(2,1)S(1)}, bf16[144,512]{1,0:T(8,128)(2,1)}, ...), branch_computations={%region_45.44_spmd, %region_46.56_spmd} | conditional | flops 307384960 | bytes 36977952 | solution.py:250
  1322.1 87.4 %conditional.12 = ((f32[3,512,512]{2,1,0:T(8,128)S(1)}, f32[3,512,512]{1,2,0:T(8,128)}, f32[3,9,512]{2,1,0:T(8,128)}, bf16[1,144,512]{2,1,0:T(8,128)(2,1)S(1)}, bf16[1,144,512]{2,1,0:T(8,128)(2,1)})) conditional(s32[]{:T(128)} %convert_element_type.275, (bf16[144,512]{1,0:T(8,128)(2,1)S(1)}, bf16[144,512]{1,0:T(8,128)(2,1)}, ...), branch_computations={%region_17.17_spmd, %region_18.57_spmd} | conditional | flops 922154880 | bytes 121950032 | solution.py:258
  1329.0 23.8 %conditional.5 = (bf16[144,512]{1,0:T(8,128)(2,1)S(1)}, bf16[144,512]{1,0:T(8,128)(2,1)}, f32[3,512,512]{2,1,0:T(8,128)S(1)}, f32[3,512,512]{1,2,0:T(8,128)}, f32[3,9,512]{2,1,0:T(8,128)}) conditional(s32[]{:T(128)} %convert_element_type.202, (bf16[144,512]{1,0:T(8,128)(2,1)S(1)}, bf16[144,512]{1,0:T(8,128)(2,1)}, f32[3,512,512]{2,1,0:T(8,128)S(1)}, ...), branch_computations={%region_19.18_spmd, %region_20.30_spmd} | conditional | flops 307384960 | bytes 38799412 | solution.py:250
  1353.5 23.7 %conditional.6 = (bf16[144,512]{1,0:T(8,128)(2,1)S(1)}, bf16[144,512]{1,0:T(8,128)(2,1)}, f32[3,512,512]{2,1,0:T(8,128)S(1)}, f32[3,512,512]{1,2,0:T(8,128)}, f32[3,9,512]{2,1,0:T(8,128)}) conditional(s32[]{:T(128)} %convert_element_type.201, (bf16[144,512]{1,0:T(8,128)(2,1)S(1)}, bf16[144,512]{1,0:T(8,128)(2,1)}, f32[3,512,512]{2,1,0:T(8,128)S(1)}, ...), branch_computations={%region_32.31_spmd, %region_33.43_spmd} | conditional | flops 307384960 | bytes 38799412 | solution.py:250
  1381.8 27.6 %conditional.7 = (f32[3,512,512]{2,1,0:T(8,128)S(1)}, f32[3,512,512]{1,2,0:T(8,128)}, f32[3,9,512]{2,1,0:T(8,128)}, bf16[1,144,512]{2,1,0:T(8,128)(2,1)S(1)}, bf16[1,144,512]{2,1,0:T(8,128)(2,1)}) conditional(s32[]{:T(128)} %convert_element_type.200, (bf16[144,512]{1,0:T(8,128)(2,1)S(1)}, bf16[144,512]{1,0:T(8,128)(2,1)}, ...), branch_computations={%region_45.44_spmd, %region_46.56_spmd} | conditional | flops 307384960 | bytes 36977952 | solution.py:250
  1426.8 133.4 %psum.23 = f32[3,9,512]{2,0,1:T(4,128)} all-reduce(f32[3,9,512]{2,0,1:T(4,128)S(1)} %copy.14), channel_id=1, replica_groups=mesh['segment'=8,'dp'=32] {'dp'}, use_global_device_ids=true, to_apply=%region_61.62 | all-reduce | flops 13824 | bytes 110592 | tf_op jit(solution)/shard_map/psum | solution.py:263
  1560.2 137.8 %all-reduce.12.cloned.1.call-done = (f32[3,512,512]{2,1,0:T(8,128)}, f32[3,512,512]{2,1,0:T(8,128)}) async-done(((f32[3,512,512]{2,1,0:T(8,128)}, f32[3,512,512]{2,1,0:T(8,128)}), (f32[3,512,512]{2,1,0:T(8,128)}, f32[3,512,512]{2,1,0:T(8,128)})) %all-reduce.12.cloned.1.call-update) | async-done | bytes 6291472 | tf_op jit(solution)/shard_map/psum | solution.py:263
  (702 shorter events, 776.2 us)
Async XLA Ops:
  7.2 1690.8 %all-reduce.12.cloned.1.call-start = ((), (), s32[]{:S(2)}) async-start(), calls=%async_computation | async-start | bytes 12582912 | tf_op jit(solution)/shard_map/psum | solution.py:263
  10.1 5.8 copy-start.7
  43.0 4.9 collective-permute-start
  75.7 9.1 collective-permute-start
  112.6 9.1 collective-permute-start
  149.4 9.1 collective-permute-start
  163.8 31.6 %collective-permute-start = (bf16[2,144,512]{2,1,0:T(8,128)(2,1)S(1)}, bf16[2,144,512]{2,1,0:T(8,128)(2,1)S(1)}, u32[]{:S(2)}, u32[]{:S(2)}) collective-permute-start(bf16[2,144,512]{2,1,0:T(8,128)(2,1)S(1)} %pad_maximum_fusion.4), channel_id=1, source_target_pairs={{0,32},{32,64},{64,96},{96,128},{128,160},{160,192},{192,224},{1,3... | collective-permute-start | bytes 884744 | tf_op jit(solution)/shard_map/while/body/eval_jaxpr/ppermute | solution.py:15
  200.6 9.1 collective-permute-start
  215.0 31.8 %collective-permute-start = (bf16[2,144,512]{2,1,0:T(8,128)(2,1)S(1)}, bf16[2,144,512]{2,1,0:T(8,128)(2,1)S(1)}, u32[]{:S(2)}, u32[]{:S(2)}) collective-permute-start(bf16[2,144,512]{2,1,0:T(8,128)(2,1)S(1)} %pad_maximum_fusion.4), channel_id=1, source_target_pairs={{0,32},{32,64},{64,96},{96,128},{128,160},{160,192},{192,224},{1,3... | collective-permute-start | bytes 884744 | tf_op jit(solution)/shard_map/while/body/eval_jaxpr/ppermute | solution.py:15
  252.0 10.0 collective-permute-start
  267.3 27.3 %collective-permute-start = (bf16[2,144,512]{2,1,0:T(8,128)(2,1)S(1)}, bf16[2,144,512]{2,1,0:T(8,128)(2,1)S(1)}, u32[]{:S(2)}, u32[]{:S(2)}) collective-permute-start(bf16[2,144,512]{2,1,0:T(8,128)(2,1)S(1)} %pad_maximum_fusion.4), channel_id=1, source_target_pairs={{0,32},{32,64},{64,96},{96,128},{128,160},{160,192},{192,224},{1,3... | collective-permute-start | bytes 884744 | tf_op jit(solution)/shard_map/while/body/eval_jaxpr/ppermute | solution.py:15
  299.8 10.0 collective-permute-start
  315.1 20.8 %collective-permute-start = (bf16[2,144,512]{2,1,0:T(8,128)(2,1)S(1)}, bf16[2,144,512]{2,1,0:T(8,128)(2,1)S(1)}, u32[]{:S(2)}, u32[]{:S(2)}) collective-permute-start(bf16[2,144,512]{2,1,0:T(8,128)(2,1)S(1)} %pad_maximum_fusion.4), channel_id=1, source_target_pairs={{0,32},{32,64},{64,96},{96,128},{128,160},{160,192},{192,224},{1,3... | collective-permute-start | bytes 884744 | tf_op jit(solution)/shard_map/while/body/eval_jaxpr/ppermute | solution.py:15
  344.5 13.0 collective-permute-start.1
  361.6 28.1 %collective-permute-start.1 = (bf16[2,144,512]{2,1,0:T(8,128)(2,1)}, bf16[2,144,512]{2,1,0:T(8,128)(2,1)S(1)}, u32[]{:S(2)}, u32[]{:S(2)}) collective-permute-start(bf16[2,144,512]{2,1,0:T(8,128)(2,1)} %pad_maximum_fusion.5), channel_id=1, source_target_pairs={{32,0},{64,32},{96,64},{128,96},{160,128},{192,160},{224,192},{33,... | collective-permute-start | bytes 884744 | tf_op jit(solution)/shard_map/while/body/eval_jaxpr/ppermute | solution.py:15
  393.8 16.5 collective-permute-start.1
  414.5 17.9 %collective-permute-start.1 = (bf16[2,144,512]{2,1,0:T(8,128)(2,1)}, bf16[2,144,512]{2,1,0:T(8,128)(2,1)S(1)}, u32[]{:S(2)}, u32[]{:S(2)}) collective-permute-start(bf16[2,144,512]{2,1,0:T(8,128)(2,1)} %pad_maximum_fusion.5), channel_id=1, source_target_pairs={{32,0},{64,32},{96,64},{128,96},{160,128},{192,160},{224,192},{33,... | collective-permute-start | bytes 884744 | tf_op jit(solution)/shard_map/while/body/eval_jaxpr/ppermute | solution.py:15
  436.5 21.7 %collective-permute-start.1 = (bf16[2,144,512]{2,1,0:T(8,128)(2,1)}, bf16[2,144,512]{2,1,0:T(8,128)(2,1)S(1)}, u32[]{:S(2)}, u32[]{:S(2)}) collective-permute-start(bf16[2,144,512]{2,1,0:T(8,128)(2,1)} %pad_maximum_fusion.5), channel_id=1, source_target_pairs={{32,0},{64,32},{96,64},{128,96},{160,128},{192,160},{224,192},{33,... | collective-permute-start | bytes 884744 | tf_op jit(solution)/shard_map/while/body/eval_jaxpr/ppermute | solution.py:15
  462.3 18.5 %collective-permute-start.1 = (bf16[2,144,512]{2,1,0:T(8,128)(2,1)}, bf16[2,144,512]{2,1,0:T(8,128)(2,1)S(1)}, u32[]{:S(2)}, u32[]{:S(2)}) collective-permute-start(bf16[2,144,512]{2,1,0:T(8,128)(2,1)} %pad_maximum_fusion.5), channel_id=1, source_target_pairs={{32,0},{64,32},{96,64},{128,96},{160,128},{192,160},{224,192},{33,... | collective-permute-start | bytes 884744 | tf_op jit(solution)/shard_map/while/body/eval_jaxpr/ppermute | solution.py:15
  484.9 529.8 %collective-permute-start.1 = (bf16[2,144,512]{2,1,0:T(8,128)(2,1)}, bf16[2,144,512]{2,1,0:T(8,128)(2,1)S(1)}, u32[]{:S(2)}, u32[]{:S(2)}) collective-permute-start(bf16[2,144,512]{2,1,0:T(8,128)(2,1)} %pad_maximum_fusion.5), channel_id=1, source_target_pairs={{32,0},{64,32},{96,64},{128,96},{160,128},{192,160},{224,192},{33,... | collective-permute-start | bytes 884744 | tf_op jit(solution)/shard_map/while/body/eval_jaxpr/ppermute | solution.py:15
  1041.6 4.4 copy-start.11
  1097.0 4.7 copy-start.5
  1106.3 10.1 collective-permute-start.1
  1143.2 4.4 copy-start.11
  1198.6 4.7 copy-start.5
  1207.9 10.1 collective-permute-start.1
  1244.8 4.4 copy-start.11
  1300.2 4.7 copy-start.5
  1309.5 10.1 collective-permute-start.1
  1401.8 4.7 copy-start.5
  1411.1 9.2 collective-permute-start.1
  1421.0 4.8 copy-start
  (46 other events, 116.3 us)
Sparse Core Ops, SparseCore 0:
  1425.9 271.9 all-reduce.11
where the time goes:
time: 1720 us; the launch traced here: 1710 us
  waiting for transfers between devices  849 us (49%)
  other arithmetic  251 us (15%)
  local copies, waits for them, and re-layouts  198 us (12%)
  starting transfers between devices  147 us (9%)
  blocking collectives  133 us (8%)
  matrix products  99.8 us (6%)
  loops' own time  18.5 us (1%)
    ppermute x22, waiting for transfers between devices, shifted(): return lax.ppermute(value, axis, pairs)  711 us
    ppermute x22, starting transfers between devices, shifted(): return lax.ppermute(value, axis, pairs)  147 us
    psum x1, waiting for transfers between devices, shards(): totals = lax.psum(carry[2], 'dp')  138 us
    psum x1, blocking collectives, shards(): totals = lax.psum(carry[2], 'dp')  133 us
  transfers between devices with their start and end apart: 23, of which 23 were waited for; matrix products, arithmetic and copies ran while one was open for 0% of the time, Pallas kernels for 0%

commit v1 on v0

v1 whole, which is shorter than its diff:
```python
import functools

import jax
import jax.numpy as jnp
from jax import lax
from jax.experimental import pallas as pl
from jax.experimental.pallas import tpu as pltpu
from jax.sharding import PartitionSpec as P

GRID = 12
PITCH = 16
ROWS = GRID * PITCH
CH = 512
CELLS = 12
EPSILON = 1e-06
MESH = pl.DeviceIdType.MESH
BF = jnp.bfloat16
F32 = jnp.float32


def place():
    seg, dp = lax.axis_index("segment"), lax.axis_index("dp")
    y, xh = seg // 2, seg % 2
    core, xl, z = dp % 2, (dp // 2) % 2, dp // 4
    return seg, dp, y, xh, z, xl, core


def dev(y, xh, z, xl, core):
    return (y * 2 + xh, (z * 2 + xl) * 2 + core)


def neighbours():
    seg, dp, y, xh, z, xl, core = place()
    yp = y + 1 - 2 * (y % 2)
    return {
        "core": dev(y, xh, z, xl, 1 - core),
        "xs": dev(y, xh, z, 1 - xl, core),
        "xd": dev(y, 1 - xh, z, 1 - xl, core),
        "x+": dev(y, jnp.where(xl == 0, xh, 1 - xh), z, 1 - xl, core),
        "x-": dev(y, jnp.where(xl == 1, xh, 1 - xh), z, 1 - xl, core),
        "z+": dev(y, xh, (z + 1) % 8, xl, core),
        "z-": dev(y, xh, (z + 7) % 8, xl, core),
        "y": dev(yp, xh, z, xl, core),
        "hop": dev(3 - y, xh, z, xl, core),
    }


def greet(names, near):
    barrier = pltpu.get_barrier_semaphore()
    for name in names:
        pl.semaphore_signal(barrier, inc=1, device_id=near[name], device_id_type=MESH)
    pl.semaphore_wait(barrier, len(names))


def remote(src, dst, send, recv, i, target):
    return pltpu.make_async_remote_copy(
        src_ref=src, dst_ref=dst, send_sem=send.at[i], recv_sem=recv.at[i], device_id=target, device_id_type=MESH
    )


def gather_kernel(mix_ref, point_ref, small_ref, w_ref, s_ref, send, recv, local):
    _, _, y, xh, z, xl, core = place()
    near = neighbours()
    yl, zp = y % 2, z % 2
    own = yl * 2 + xh
    sec_y, sec_x, sec_xy = (1 - yl) * 2 + xh, yl * 2 + (1 - xh), (1 - yl) * 2 + (1 - xh)
    loc = [
        pltpu.make_async_copy(mix_ref, w_ref.at[0, pl.ds(own * 3, 3)], local.at[0]),
        pltpu.make_async_copy(point_ref, w_ref.at[1, pl.ds(own * 3, 3)], local.at[1]),
        pltpu.make_async_copy(small_ref, s_ref.at[pl.ds(own * 3, 3)], local.at[2]),
    ]
    for c in loc:
        c.start()
    greet(("core", "xs", "xd", "z+", "z-", "y"), near)
    for c in loc:
        c.wait()

    def piece(i, sec, row, count, name):
        at = w_ref.at[core, pl.ds(sec * 3, 3), pl.ds(pl.multiple_of(row, 16), count)]
        return remote(at, at, send, recv, i, near[name])

    def tiny(i, sec, name):
        at = s_ref.at[pl.ds(sec * 3, 3)]
        return remote(at, at, send, recv, i, near[name])

    mine, other = 128 * (2 * zp + xl), 128 * (2 * zp + 1 - xl)
    t = {
        0: piece(0, own, 256 * zp, 256, "y"),
        1: piece(1, own, other, 128, "xd"),
        2: piece(2, sec_x, mine, 128, "xs"),
        3: piece(3, sec_x, mine, 64, "z+"),
        4: piece(4, sec_x, mine + 64, 64, "z-"),
        5: piece(5, sec_y, other, 128, "xd"),
        6: piece(6, sec_y, 256 * zp, 128, "z+"),
        7: piece(7, sec_y, 256 * zp + 128, 128, "z-"),
        8: piece(8, sec_xy, mine, 128, "xs"),
        9: piece(9, sec_xy, mine, 64, "z+"),
        10: piece(10, sec_xy, mine + 64, 64, "z-"),
        11: piece(11, sec_x, other, 64, "z+"),
        12: piece(12, sec_x, other + 64, 64, "z-"),
        13: piece(13, sec_xy, other, 64, "z+"),
        14: piece(14, sec_xy, other + 64, 64, "z-"),
        15: piece(15, sec_y, 256 * zp, 256, "core"),
        16: piece(16, sec_y, 256 * (1 - zp), 256, "core"),
        17: piece(17, sec_x, 256 * zp, 256, "core"),
        18: piece(18, sec_x, 256 * (1 - zp), 256, "core"),
        19: piece(19, sec_xy, 256 * zp, 256, "core"),
        20: piece(20, sec_xy, 256 * (1 - zp), 256, "core"),
        21: tiny(21, own, "y"),
        22: tiny(22, own, "xd"),
        23: tiny(23, sec_y, "xd"),
    }

    def go(*ids):
        for i in ids:
            t[i].start()

    def got(*ids):
        for i in ids:
            t[i].wait_recv()

    go(21, 22, 1, 0)
    got(21)
    go(23)
    got(1)
    go(2, 3, 4)
    got(0)
    go(5, 6, 7, 15)
    got(2)
    go(11, 12, 17)
    got(5)
    go(8, 9, 10)
    got(6, 7)
    go(16)
    got(8)
    go(13, 14, 19)
    got(3, 4, 11, 12)
    go(18)
    got(9, 10, 13, 14)
    go(20)
    got(22, 23, 15, 16, 17, 18, 19, 20)
    for i in range(24):
        t[i].wait_send()


def gather(w_mix, w_point, small):
    return pl.pallas_call(
        gather_kernel,
        out_shape=(
            jax.ShapeDtypeStruct((2, CELLS, CH, CH), BF),
            jax.ShapeDtypeStruct((CELLS, 16, CH), BF),
        ),
        in_specs=[pl.BlockSpec(memory_space=pl.ANY)] * 3,
        out_specs=(pl.BlockSpec(memory_space=pl.ANY),) * 2,
        scratch_shapes=[
            pltpu.SemaphoreType.DMA((24,)),
            pltpu.SemaphoreType.DMA((24,)),
            pltpu.SemaphoreType.DMA((3,)),
        ],
        compiler_params=pltpu.CompilerParams(collective_id=1, has_side_effects=True),
        name="gather",
    )(w_mix, w_point, small)


def hop_kernel(x_ref, o_ref, send, recv):
    near = neighbours()
    greet(("hop",), near)
    copies = [remote(x_ref.at[i], o_ref.at[i], send, recv, i, near["hop"]) for i in range(2)]
    for c in copies:
        c.start()
    for c in copies:
        c.wait()


def hop(x):
    return pl.pallas_call(
        hop_kernel,
        out_shape=jax.ShapeDtypeStruct(x.shape, x.dtype),
        in_specs=[pl.BlockSpec(memory_space=pl.ANY)],
        out_specs=pl.BlockSpec(memory_space=pl.ANY),
        scratch_shapes=[pltpu.SemaphoreType.DMA((2,)), pltpu.SemaphoreType.DMA((2,))],
        compiler_params=pltpu.CompilerParams(collective_id=2, has_side_effects=True),
        name="hop",
    )(x)


def down(r):
    return jnp.concatenate([jnp.zeros((PITCH, r.shape[1]), r.dtype), r[:-PITCH]], axis=0)


def up(r):
    return jnp.concatenate([r[PITCH:], jnp.zeros((PITCH, r.shape[1]), r.dtype)], axis=0)


def fwd_kernel(save, flags, xa_ref, xb_ref, w_ref, k_ref, *rest):
    if save:
        c_ref, o_ref, sp_ref, so_ref, ss_ref, st_ref, hg_ref, sep = rest
    else:
        o_ref, sep = rest
    i = pl.program_id(0)

    @pl.when(i == 0)
    def _():
        @pl.when(flags[CELLS] == 0)
        def _():
            o_ref[0] = xa_ref[...]
            o_ref[1] = xa_ref[...]

        @pl.when(flags[CELLS] != 0)
        def _():
            o_ref[...] = xb_ref[...]

    @pl.when(flags[i] == 1)
    def _():
        if save:
            sp_ref[0] = o_ref[0]
            so_ref[0] = o_ref[1]
        real = lax.broadcasted_iota(jnp.int32, (ROWS, 128), 0) % PITCH < GRID
        for c in range(4):
            cols = slice(128 * c, 128 * c + 128)
            a = jnp.maximum(o_ref[1, :, cols].astype(F32), 0.0)
            k = k_ref[0, :, cols].astype(F32)
            am, ap = pltpu.roll(a, 1, 0), pltpu.roll(a, ROWS - 1, 0)
            r = [k[3 * u : 3 * u + 1] * am + k[3 * u + 1 : 3 * u + 2] * a + k[3 * u + 2 : 3 * u + 3] * ap for u in range(3)]
            s = r[1] + down(r[0]) + up(r[2])
            sep[:, cols] = jnp.where(real, s, 0.0).astype(BF)
        if save:
            ss_ref[0] = sep[...]
        prev = o_ref[0]
        total = jnp.dot(sep[...], w_ref[1, 0], preferred_element_type=F32)
        total = total + jnp.dot(jnp.maximum(prev, 0), w_ref[0, 0], preferred_element_type=F32)
        total = prev.astype(F32) + total
        q = lax.rsqrt(jnp.mean(total * total, axis=-1, keepdims=True) + EPSILON)
        if save:
            st_ref[0] = total
        o_ref[1] = prev
        o_ref[0] = (total * q).astype(BF)

    if save:

        @pl.when(i == CELLS - 1)
        def _():
            last = o_ref[0]
            pooled = jnp.sum(jnp.maximum(last.astype(F32), 0.0), axis=0, keepdims=True) / (GRID * GRID)
            grad = jnp.zeros((1, CH), F32)
            for k in range(4):
                row = c_ref[k : k + 1, :]
                logit = jnp.sum(pooled * row, axis=-1, keepdims=True)
                hot = jnp.where(flags[CELLS + 1] == k, 1.0, 0.0)
                grad = grad + (logit - hot) * row
            grad = grad / (GRID * GRID)
            hg_ref[0] = jnp.where(last > 0, jnp.broadcast_to(grad, last.shape), 0.0).astype(BF)
            hg_ref[1] = jnp.zeros((ROWS, CH), BF)


def forward(flags, image, arrived, weights, small, classes, save):
    whole = lambda n: pl.BlockSpec(n, lambda i, f: (0,) * len(n))
    one = lambda n: pl.BlockSpec((1,) + n, lambda i, f: (i, 0, 0))
    pair = jax.ShapeDtypeStruct((2, ROWS, CH), BF)
    in_specs = [
        whole((ROWS, CH)),
        whole((2, ROWS, CH)),
        pl.BlockSpec((2, 1, CH, CH), lambda i, f: (0, i, 0, 0)),
        one((16, CH)),
    ]
    out_specs, out_shape = [whole((2, ROWS, CH))], [pair]
    args = [flags, image, arrived, weights, small]
    if save:
        in_specs.append(whole((8, CH)))
        args.append(classes)
        out_specs += [one((ROWS, CH))] * 4 + [whole((2, ROWS, CH))]
        kept = jax.ShapeDtypeStruct((CELLS, ROWS, CH), BF)
        out_shape += [kept, kept, kept, jax.ShapeDtypeStruct((CELLS, ROWS, CH), F32), pair]
    return pl.pallas_call(
        functools.partial(fwd_kernel, save),
        grid_spec=pltpu.PrefetchScalarGridSpec(
            num_scalar_prefetch=1,
            grid=(CELLS,),
            in_specs=in_specs,
            out_specs=out_specs,
            scratch_shapes=[pltpu.VMEM((ROWS, CH), BF)],
        ),
        out_shape=out_shape,
        compiler_params=pltpu.CompilerParams(vmem_limit_bytes=32 << 20),
        name="forward_save" if save else "forward",
    )(*args)


NT = (((1,), (1,)), ((), ()))
TN = (((0,), (0,)), ((), ()))


def bwd_kernel(wgrad, flags, ga_ref, gb_ref, w_ref, k_ref, sp_ref, so_ref, ss_ref, st_ref, *rest):
    if wgrad:
        gw_ref, gk_ref, o_ref, gs = rest
    else:
        o_ref, gs = rest
    i = pl.program_id(0)
    cell = CELLS - 1 - i

    @pl.when(i == 0)
    def _():
        @pl.when(flags[CELLS] == 0)
        def _():
            o_ref[...] = ga_ref[...]

        @pl.when(flags[CELLS] != 0)
        def _():
            o_ref[...] = gb_ref[...]

    @pl.when(flags[cell] == 1)
    def _():
        total = st_ref[0]
        q = lax.rsqrt(jnp.mean(total * total, axis=-1, keepdims=True) + EPSILON)
        n = total * q
        gn = o_ref[0].astype(F32)
        gt = q * (gn - n * jnp.mean(gn * n, axis=-1, keepdims=True))
        gh = gt.astype(BF)
        gs[...] = lax.dot_general(gh, w_ref[1, 0], NT, preferred_element_type=F32)
        gm = lax.dot_general(gh, w_ref[0, 0], NT, preferred_element_type=F32)
        prev = sp_ref[0]
        o_ref[0] = (gt + jnp.where(prev > 0, gm, 0.0) + o_ref[1].astype(F32)).astype(BF)
        for c in range(4):
            cols = slice(128 * c, 128 * c + 128)
            g = gs[:, cols]
            k = k_ref[0, :, cols].astype(F32)
            gv = [pltpu.roll(g, ROWS - 1, 0), g, pltpu.roll(g, 1, 0)]
            r = [
                k[3 * u : 3 * u + 1] * gv[0] + k[3 * u + 1 : 3 * u + 2] * gv[1] + k[3 * u + 2 : 3 * u + 3] * gv[2]
                for u in range(3)
            ]
            rel = r[1] + up(r[0]) + down(r[2])
            older = so_ref[0, :, cols]
            o_ref[1, :, cols] = jnp.where(older > 0, rel, 0.0).astype(BF)
            if wgrad:
                a = jnp.maximum(older.astype(F32), 0.0)
                for v in range(3):
                    gk_ref[0, v : v + 1, cols] = jnp.sum(a[:-PITCH] * gv[v][PITCH:], axis=0, keepdims=True)
                    gk_ref[0, 3 + v : 4 + v, cols] = jnp.sum(a * gv[v], axis=0, keepdims=True)
                    gk_ref[0, 6 + v : 7 + v, cols] = jnp.sum(a[PITCH:] * gv[v][:-PITCH], axis=0, keepdims=True)
        if wgrad:
            gw_ref[0, 0] = lax.dot_general(jnp.maximum(prev, 0), gh, TN, preferred_element_type=F32).astype(BF)
            gw_ref[1, 0] = lax.dot_general(ss_ref[0], gh, TN, preferred_element_type=F32).astype(BF)

    if wgrad:

        @pl.when(flags[cell] != 1)
        def _():
            gw_ref[...] = jnp.zeros_like(gw_ref)
            gk_ref[...] = jnp.zeros_like(gk_ref)


def backward(flags, arrived, head, weights, small, saved, wgrad):
    whole = lambda n: pl.BlockSpec(n, lambda i, f: (0,) * len(n))
    one = lambda n: pl.BlockSpec((1,) + n, lambda i, f: (CELLS - 1 - i, 0, 0))
    both = pl.BlockSpec((2, 1, CH, CH), lambda i, f: (0, CELLS - 1 - i, 0, 0))
    out_specs, out_shape = [whole((2, ROWS, CH))], [jax.ShapeDtypeStruct((2, ROWS, CH), BF)]
    if wgrad:
        out_specs = [both, one((16, CH))] + out_specs
        out_shape = [
            jax.ShapeDtypeStruct((2, CELLS, CH, CH), BF),
            jax.ShapeDtypeStruct((CELLS, 16, CH), F32),
        ] + out_shape
    return pl.pallas_call(
        functools.partial(bwd_kernel, wgrad),
        grid_spec=pltpu.PrefetchScalarGridSpec(
            num_scalar_prefetch=1,
            grid=(CELLS,),
            in_specs=[whole((2, ROWS, CH)), whole((2, ROWS, CH)), both, one((16, CH))] + [one((ROWS, CH))] * 4,
            out_specs=out_specs,
            scratch_shapes=[pltpu.VMEM((ROWS, CH), F32)],
        ),
        out_shape=out_shape,
        compiler_params=pltpu.CompilerParams(vmem_limit_bytes=32 << 20),
        name="backward_weights" if wgrad else "backward",
    )(flags, arrived, head, weights, small, *saved)


def sum_kernel(g_ref, o_ref, acc, rb, zp0, zp, xp0, xp, ap0, ap, bp0, bp, yb, ob, send, recv, local):
    _, _, y, xh, z, xl, core = place()
    near = neighbours()
    yl = y % 2
    count = [0]
    sends = []

    def move(src, dst, name):
        c = remote(src, dst, send, recv, count[0], near[name])
        count[0] += 1
        sends.append(c)
        c.start()
        return c

    load = pltpu.make_async_copy(g_ref.at[core], acc, local.at[0])
    load.start()
    greet(("core", "xs", "xd", "z+", "z-", "y"), near)
    twin = [move(g_ref.at[1 - core, a, b], rb.at[a, b], "core") for a in range(2) for b in range(2)]
    load.wait()
    for j in range(4):
        a, b = j // 2, j % 2
        twin[j].wait_recv()

        def add(n, _, a=a, b=b):
            s, zz = n // 8, n % 8
            acc[a, b, s, zz] = (acc[a, b, s, zz].astype(F32) + rb[a, b, s, zz].astype(F32)).astype(BF)
            return 0

        lax.fori_loop(0, 24, add, 0)

    def plus(ref, *others):
        def step(s, _):
            v = ref[:, s].astype(F32)
            for o in others:
                v = v + o[:, s].astype(F32)
            ref[:, s] = v.astype(BF)
            return 0

        lax.fori_loop(0, 3, step, 0)

    def zat(d):
        return (z + 8 + d) % 8

    def xat(d):
        x = (xh * 2 + xl + 4 + d) % 4
        return x // 2, x % 2

    def a1(d):
        return acc.at[:, :, :, zat(d), 0]

    def b1(d):
        h, l = xat(d)
        return acc.at[:, h, :, :, 1, l]

    def a2(d):
        h, l = xat(d)
        return acc.at[:, h, :, z, 0, l]

    def b2(d):
        return acc.at[:, xh, :, zat(d), 1, xl]

    def plus4(ref, *others):
        def step(n, _):
            a, b = n // 2, n % 2
            v = ref[a, b].astype(F32)
            for o in others:
                v = v + o[a, b].astype(F32)
            ref[a, b] = v.astype(BF)
            return 0

        lax.fori_loop(0, 4, step, 0)

    za = [move(a1(4).at[:, :, :, 0], zp0.at[0], "z+"), move(a1(4).at[:, :, :, 1], zp0.at[1], "z-")]
    xa = [move(b1(2).at[0], xp0.at[0], "x+"), move(b1(2).at[1], xp0.at[1], "x-")]

    for c in za:
        c.wait_recv()
    plus4(a1(3).at[:, :, :, 0], zp0.at[0])
    plus4(a1(-3).at[:, :, :, 1], zp0.at[1])
    za = [move(a1(3), zp.at[0, 0], "z+"), move(a1(-3), zp.at[0, 1], "z-")]

    for c in xa:
        c.wait_recv()

    def plus1(ref, other):
        def step(s, _):
            ref[s] = (ref[s].astype(F32) + other[s].astype(F32)).astype(BF)
            return 0

        lax.fori_loop(0, 3, step, 0)

    plus1(b1(1).at[0], xp0.at[0])
    plus1(b1(-1).at[1], xp0.at[1])
    xa = [move(b1(1), xp.at[0], "x+"), move(b1(-1), xp.at[1], "x-")]

    for k in (2, 1):
        for c in za:
            c.wait_recv()
        plus4(a1(k), zp.at[2 - k, 0])
        plus4(a1(-k), zp.at[2 - k, 1])
        za = [move(a1(k), zp.at[3 - k, 0], "z+"), move(a1(-k), zp.at[3 - k, 1], "z-")]

    for c in xa:
        c.wait_recv()
    plus(b1(0), xp.at[0], xp.at[1])
    zb = [move(b2(4).at[0], bp0.at[0], "z+"), move(b2(4).at[1], bp0.at[1], "z-")]

    for c in za:
        c.wait_recv()
    plus4(a1(0), zp.at[2, 0], zp.at[2, 1])
    xb = [move(a2(2).at[0], ap0.at[0], "x+"), move(a2(2).at[1], ap0.at[1], "x-")]

    for c in zb:
        c.wait_recv()
    plus1(b2(3).at[0], bp0.at[0])
    plus1(b2(-3).at[1], bp0.at[1])
    zb = [move(b2(3), bp.at[0, 0], "z+"), move(b2(-3), bp.at[0, 1], "z-")]

    for c in xb:
        c.wait_recv()
    plus1(a2(1).at[0], ap0.at[0])
    plus1(a2(-1).at[1], ap0.at[1])
    xb = [move(a2(1), ap.at[0], "x+"), move(a2(-1), ap.at[1], "x-")]

    for k in (2, 1):
        for c in zb:
            c.wait_recv()
        plus(b2(k), bp.at[2 - k, 0])
        plus(b2(-k), bp.at[2 - k, 1])
        zb = [move(b2(k), bp.at[3 - k, 0], "z+"), move(b2(-k), bp.at[3 - k, 1], "z-")]
    for c in xb:
        c.wait_recv()
    plus(a2(0), ap.at[0], ap.at[1])
    ya = [move(acc.at[1 - yl, xh, :, z, 0, xl], yb.at[0], "y")]
    for c in zb:
        c.wait_recv()
    plus(b2(0), bp.at[2, 0], bp.at[2, 1])
    ya.append(move(acc.at[1 - yl, xh, :, z, 1, xl], yb.at[1], "y"))
    for c in range(2):
        ya[c].wait_recv()
        for s in range(3):
            ob[core, s, z, c, xl] = (acc[yl, xh, s, z, c, xl].astype(F32) + yb[c, s].astype(F32)).astype(BF)

    def both_cores(at):
        return move(at, at, "core")

    mine = ob.at[core, :, z, :, xl]
    pair = move(mine, mine, "xs")
    pair.wait_recv()
    chunk = lambda d: ob.at[core, :, zat(d)]
    last = [both_cores(chunk(0))]
    out = [move(chunk(0), chunk(0), "z+"), move(chunk(0), chunk(0), "z-")]
    for k in (1, 2):
        for c in out:
            c.wait_recv()
        out = [move(chunk(-k), chunk(-k), "z+"), move(chunk(k), chunk(k), "z-")]
        last += [both_cores(chunk(-k)), both_cores(chunk(k))]
    for c in out:
        c.wait_recv()
    out = [
        move(chunk(-3).at[:, 0], chunk(-3).at[:, 0], "z+"),
        move(chunk(3).at[:, 1], chunk(3).at[:, 1], "z-"),
    ]
    last += [both_cores(chunk(-3)), both_cores(chunk(3))]
    for c in out:
        c.wait_recv()
    last += [both_cores(chunk(4))]
    for c in last:
        c.wait_recv()
    for c in sends:
        c.wait_send()
    done = pltpu.make_async_copy(ob, o_ref, local.at[0])
    done.start()
    done.wait()


def sum_up(grads):
    n = 64
    lead = (16, CH)
    shape = lambda *d: pltpu.VMEM(d + lead, BF)
    return pl.pallas_call(
        sum_kernel,
        out_shape=jax.ShapeDtypeStruct((2, 3, 8, 2, 2, 16, CH), BF),
        in_specs=[pl.BlockSpec(memory_space=pl.ANY)],
        out_specs=pl.BlockSpec(memory_space=pl.ANY),
        scratch_shapes=[
            shape(2, 2, 3, 8, 2, 2),
            shape(2, 2, 3, 8, 2, 2),
            shape(2, 2, 2, 3),
            shape(3, 2, 2, 2, 3, 2),
            shape(2, 3, 8),
            shape(2, 2, 3, 8),
            shape(2, 3),
            shape(2, 2, 3),
            shape(2, 3),
            shape(3, 2, 2, 3),
            shape(2, 3),
            shape(2, 3, 8, 2, 2),
            pltpu.SemaphoreType.DMA((n,)),
            pltpu.SemaphoreType.DMA((n,)),
            pltpu.SemaphoreType.DMA((1,)),
        ],
        compiler_params=pltpu.CompilerParams(collective_id=3, has_side_effects=True, vmem_limit_bytes=48 << 20),
        name="sum_up",
    )(grads)


def shards(features, labels, classifier, w_mix, w_point, kernels, counts):
    _, _, y, xh, z, xl, core = place()
    stage = y // 2
    image = jnp.where(stage == 0, y, 3 - y) * 2 + xh
    tail = jnp.broadcast_to(counts[0].astype(BF), (3, 7, CH))
    small = jnp.concatenate([kernels, tail], axis=1)
    weights, smalls = gather(w_mix, w_point, small)
    active = (jnp.arange(CELLS) % 3).astype(F32) < smalls[:, 9, 0].astype(F32)
    label = lax.dynamic_index_in_dim(labels, image, 0, keepdims=False)
    flags = jnp.concatenate([active.astype(jnp.int32), jnp.stack([stage, label]).astype(jnp.int32)])
    first = jnp.concatenate([active.astype(jnp.int32), jnp.zeros((2,), jnp.int32)])
    own = lax.dynamic_index_in_dim(features, image, 0, keepdims=False).reshape(GRID, GRID, CH)
    own = jnp.pad(own, ((0, 0), (0, PITCH - GRID), (0, 0))).reshape(ROWS, CH)
    classes = jnp.pad(classifier.T, ((0, 4), (0, 0)))

    (half,) = forward(first, own, jnp.zeros((2, ROWS, CH), BF), weights, smalls, None, False)
    arrived = hop(half)
    _, *saved, head = forward(flags, own, arrived, weights, smalls, classes, True)
    (back,) = backward(flags, head, head, weights, smalls, saved, False)
    arrived = hop(back)
    grads, kernel_grads, _ = backward(flags, arrived, head, weights, smalls, saved, True)
    summed = sum_up(grads.reshape(2, 2, 2, 3, 8, 2, 2, 16, CH))
    summed = summed.reshape(2, 3, CH, CH).astype(F32)

    mine = kernel_grads[:, :9]
    wide = jnp.zeros((2, CELLS, 9, CH), F32)
    wide = lax.dynamic_update_index_in_dim(wide, mine, stage, 0).reshape(24, 9, CH)
    wide = lax.psum(wide, ("segment", "dp"))
    tap = lax.dynamic_slice_in_dim(wide, (y * 2 + xh) * 3, 3, 0)
    return summed[0], summed[1], tap


def solution(mesh):
    return jax.shard_map(
        shards,
        mesh=mesh,
        in_specs=(
            P("dp", None, None),
            P("dp"),
            P(),
            P("segment", None, None),
            P("segment", None, None),
            P("segment", None, None),
            P("segment"),
        ),
        out_specs=(P("segment", None, None), P("segment", None, None), P("segment", None, None)),
        check_vma=False,
    )
```

time: 1720 us -> 525 us (0.31)
  waiting for transfers between devices: 849 us -> 142 us
  Pallas kernels: 0 us -> 333 us
  other arithmetic: 251 us -> 1.67 us
  local copies, waits for them, and re-layouts: 198 us -> 32.4 us
  starting transfers between devices: 147 us -> 0.04 us
  blocking collectives: 133 us -> 0 us
  matrix products: 99.8 us -> 0 us
  loops' own time: 18.5 us -> 0 us
    ppermute x22 -> x0, waiting for transfers between devices: 711 us -> none  [shifted(): return lax.ppermute(value, axis, pairs)]
    pallas_call x0 -> x8, Pallas kernels: none -> 333 us  [the longest x1 152 us: gather(): pl.pallas_call(gather_kernel, out_shape=(jax.ShapeDtypeStruct((2, CELLS,...]
    ppermute x22 -> x0, starting transfers between devices: 147 us -> none  [shifted(): return lax.ppermute(value, axis, pairs)]
    psum x1 -> x0, blocking collectives: 133 us -> none  [shards(): totals = lax.psum(carry[2], 'dp')]
    dot_general x72 -> x0, matrix products: 99.8 us -> none  [the longest x12 30.9 us: cell_backward(): jnp.dot(grad_half, point_weight.T, preferred_element_type=jnp.float32)]
    reduce_sum x32 -> x0, other arithmetic: 59.5 us -> none  [the longest x8 32.6 us: depthwise_back(): tap_grads.append(jnp.sum(window * upstream_img, axis=summed_axes))]
    convert_element_type x68 -> x2, other arithmetic: 48.8 us -> 0.93 us  [the longest x1 0.91 us: shards(): active = (jnp.arange(CELLS) % 3).astype(F32) < smalls[:, 9, 0].astype(F32)]
    squeeze x34 -> x0, local copies, waits for them, and re-layouts: 41.5 us -> none  [the longest x4 8.93 us: load(): pairs = lax.dynamic_index_in_dim(store[0], batch_pos, 0, keepdims=False)]
  transfers between devices with their start and end apart: 23 -> 1, of which waited for: 23 -> 1; matrix products, arithmetic and copies ran while one was open for 0% -> 1% of each run, Pallas kernels for 0% -> 19%
where the time goes in v1:
time: 525 us; the launch traced here: 524 us
  Pallas kernels  333 us (63%)
  waiting for transfers between devices  142 us (27%)
  local copies, waits for them, and re-layouts  32.4 us (6%)
  between operations  15 us (3%)
    pallas_call x1, Pallas kernels, gather(): pl.pallas_call(gather_kernel, out_shape=(jax.ShapeDtypeStruct((2, CELLS,...  152 us
    psum x1, waiting for transfers between devices, shards(): wide = lax.psum(wide, ('segment', 'dp'))  142 us
    pallas_call x1, Pallas kernels, sum_up(): pl.pallas_call(sum_kernel, out_shape=jax.ShapeDtypeStruct((2, 3, 8, 2, 2,...  99.8 us
    pallas_call x2, Pallas kernels, backward(): pl.pallas_call(functools.partial(bwd_kernel, wgrad), grid_spec=pltpu.Pref...  35 us
    pallas_call x2, Pallas kernels, hop(): pl.pallas_call(hop_kernel, out_shape=jax.ShapeDtypeStruct(x.shape, x.dtyp...  23.6 us
    unnamed x39, local copies, waits for them, and re-layouts  22.9 us
    pallas_call x2, Pallas kernels, forward(): pl.pallas_call(functools.partial(fwd_kernel, save), grid_spec=pltpu.Prefe...  22.5 us
  transfers between devices with their start and end apart: 1, of which 1 were waited for; matrix products, arithmetic and copies ran while one was open for 1% of the time, Pallas kernels for 19%

profile of v1, /device:TPU:1, one launch (start us, length us, event | category | flops | bytes accessed | tf_op | source)
XLA Modules:
  0.0 524.1 jit_solution(17670162258762582420)
XLA Ops:
  7.3 0.8 copy.12
  8.7 0.6 concatenate.9.small_ref
  9.4 152.4 %gather.1 = (bf16[2,12,512,512]{3,2,1,0:T(8,128)(2,1)}, bf16[12,16,512]{2,1,0:T(8,128)(2,1)}) custom-call(bf16[3,512,512]{2,1,0:T(8,128)(2,1)} %mix_ref.1, bf16[3,512,512]{2,1,0:T(8,128)(2,1)} %point_ref.1, bf16[3,16,512]{2,1,0:T(8,128)(2,1)} %concatenate.9.small_ref), custom_call_target="tpu_custom_call" | custom-call | tf_op jit(solution)/shard_map/gather/pallas_call | solution.py:147
  161.7 0.9 convert_reduce_fusion
  162.7 0.6 dynamic_slice.11
  163.4 0.7 fusion.2
  164.2 4.6 copy-done.1
  168.7 0.9 copy-done.9
  169.7 9.1 %forward.1.x_ref = bf16[2,192,512]{2,1,0:T(8,128)(2,1)S(1)} custom-call(s32[14]{0:T(128)S(1)} %get-tuple-element.23.flags, bf16[192,512]{1,0:T(8,128)(2,1)S(1)} %bitcast.11, bf16[2,192,512]{2,1,0:T(8,128)(2,1)S(1)} %broadcast_in_dim.11.xb_ref, bf16[2,12,512,512]{3,2,1,0:T(8,128)(2,1)S(1)} %copy-done.1, bf16[12,16,512]{2,1,0:T(8,128)(2,1)S(1)} %copy-done.9), custom_call_target="tpu_custom_call" | custom-call | tf_op jit(solution)/shard_map/forward/pallas_call | solution.py:274
  178.8 0.7 copy-done.13
  179.6 12.2 %hop.2.xb_ref = bf16[2,192,512]{2,1,0:T(8,128)(2,1)} custom-call(bf16[2,192,512]{2,1,0:T(8,128)(2,1)} %copy-done.13), custom_call_target="tpu_custom_call" | custom-call | tf_op jit(solution)/shard_map/hop/pallas_call | solution.py:176
  191.9 0.9 copy-done.12
  192.8 1.0 copy-done.15
  193.8 13.4 %forward_save.1 = (bf16[2,192,512]{2,1,0:T(8,128)(2,1)}, bf16[12,192,512]{2,1,0:T(8,128)(2,1)S(1)}, bf16[12,192,512]{2,1,0:T(8,128)(2,1)S(1)}, bf16[12,192,512]{...) custom-call(s32[14]{0:T(128)S(1)} %get-tuple-element.24.flags, ...), custom_call_target="tpu_custom_call" | custom-call | tf_op jit(solution)/shard_map/forward_save/pallas_call | solution.py:274
  207.2 14.2 %backward.1.x_ref = bf16[2,192,512]{2,1,0:T(8,128)(2,1)S(1)} custom-call(s32[14]{0:T(128)S(1)} %get-tuple-element.24.flags, bf16[2,192,512]{2,1,0:T(8,128)(2,1)S(1)} %get-tuple-element.14.ga_ref.gb_ref, bf16[2,192,512]{2,1,0:T(8,128)(2,1)S(1)} %get-tuple-element.14.ga_ref.gb_ref, bf16[2,12,512,512]{3,2,1,0:T(8,128)(2,1)} %get-tuple-element.13.w_ref, ...), custom_call_target="tpu_custom_call" | custom-call | tf_op jit(solution)/shard_map/backward/pallas_call | solution.py:364
  221.4 2.1 copy-done.3
  223.5 1.4 copy-done.5
  224.9 1.4 copy-done.7
  226.3 0.8 copy-done.16
  227.1 11.3 %hop.3.ga_ref = bf16[2,192,512]{2,1,0:T(8,128)(2,1)} custom-call(bf16[2,192,512]{2,1,0:T(8,128)(2,1)} %copy-done.16), custom_call_target="tpu_custom_call" | custom-call | tf_op jit(solution)/shard_map/hop/pallas_call | solution.py:176
  238.4 2.3 copy-done.4
  240.7 1.7 copy-done.6
  242.4 1.7 copy-done.8
  244.0 1.0 copy-done.14
  245.0 20.8 %backward_weights.1 = (bf16[2,12,512,512]{3,2,1,0:T(8,128)(2,1)}, f32[12,16,512]{2,1,0:T(8,128)S(1)}, bf16[2,192,512]{2,1,0:T(8,128)(2,1)}) custom-call(s32[14]{0:T(128)S(1)} %get-tuple-element.24.flags, bf16[2,192,512]{2,1,0:T(8,128)(2,1)S(1)} %copy-done.14, bf16[2,192,512]{2,1,0:T(8,128)(2,1)S(1)} %get-tuple-element.14.ga_ref.gb_ref, ...), custom_call_target="tpu_custom_call" | custom-call | tf_op jit(solution)/shard_map/backward_weights/pallas_call | solution.py:364
  266.0 0.1 copy_dynamic-update-slice_fusion
  266.1 0.8 reshape.31
  267.0 99.8 %sum_up.1 = bf16[2,3,8,2,2,16,512]{6,5,4,3,2,1,0:T(8,128)(2,1)S(1)} custom-call(bf16[2,2,2,3,8,2,2,16,512]{8,7,6,5,4,3,2,1,0:T(8,128)(2,1)} %bitcast.13), custom_call_target="tpu_custom_call" | custom-call | tf_op jit(solution)/shard_map/sum_up/pallas_call | solution.py:559
  366.8 1.6 copy-done.2
  368.4 5.5 %fusion.1 = (f32[1,3,8,2,2,16,512]{6,5,4,3,2,1,0:T(8,128)}, f32[1,3,8,2,2,16,512]{6,5,4,3,2,1,0:T(8,128)}) fusion(bf16[2,3,8,2,2,16,512]{6,5,4,3,2,1,0:T(8,128)(2,1)} %copy-done.2), kind=kLoop, calls=%fused_computation.9 | loop fusion | bytes 12582912 | tf_op jit(solution)/shard_map/slice | solution.py:615
  373.9 141.7 %all-reduce.6.cloned.1.call-done = f32[24,9,512]{2,0,1:T(8,128)} async-done(((f32[24,9,512]{2,0,1:T(8,128)}), f32[24,9,512]{2,0,1:T(8,128)}) %all-reduce.6.cloned.1.call-update) | async-done | bytes 442384 | tf_op jit(solution)/shard_map/psum | solution.py:613
  515.6 1.6 constant_dynamic-slice_fusion
  (34 shorter events, 0.3 us)
Async XLA Ops:
  7.2 156.1 %copy-start = (bf16[4,144,512]{2,1,0:T(8,128)(2,1)S(1)}, bf16[4,144,512]{2,1,0:T(8,128)(2,1)}, u32[]{:S(2)}) copy-start(bf16[4,144,512]{2,1,0:T(8,128)(2,1)} %param.7) | copy-start | bytes 1769476
  7.2 155.5 %copy-start.18 = (s32[4]{0:T(128)S(1)}, s32[4]{0:T(128)}, u32[]{:S(2)}) copy-start(s32[4]{0:T(128)} %param.8) | copy-start | bytes 52
  7.2 508.4 %all-reduce.6.cloned.1.call-start = ((), (), s32[]{:S(2)}) async-start(), calls=%async_computation | async-start | bytes 884736 | tf_op jit(solution)/shard_map/psum | solution.py:613
  163.4 0.8 copy-start.11
  164.2 4.6 copy-start.1
  168.7 0.9 copy-start.9
  169.7 22.1 %copy-start.17 = (f32[512,4]{0,1:T(4,128)S(1)}, f32[512,4]{0,1:T(4,128)}, u32[]{:S(2)}) copy-start(f32[512,4]{0,1:T(4,128)} %param.9) | copy-start | bytes 24580
  169.7 22.2 %copy-start.10 = (bf16[12,16,512]{2,1,0:T(8,128)(2,1)S(1)}, bf16[12,16,512]{2,1,0:T(8,128)(2,1)}, u32[]{:S(2)}) copy-start(bf16[12,16,512]{2,1,0:T(8,128)(2,1)} %get-tuple-element.12.k_ref) | copy-start | bytes 589828
  178.8 0.7 copy-start.13
  191.8 0.9 copy-start.12
  192.8 1.0 copy-start.15
  221.4 2.1 copy-start.3
  223.5 1.4 copy-start.5
  224.9 1.4 copy-start.7
  226.3 0.8 copy-start.16
  238.4 2.3 copy-start.4
  240.7 1.7 copy-start.6
  242.4 1.7 copy-start.8
  244.0 1.0 copy-start.14
  366.8 1.7 copy-start.2
Sparse Core Ops, SparseCore 0:
  267.1 248.4 all-reduce.5

commit v2 on v1

--- a/solution.py
+++ b/solution.py
@@ -75,72 +75,67 @@
     for c in loc:
         c.wait()
 
-    def piece(i, sec, row, count, name):
-        at = w_ref.at[core, pl.ds(sec * 3, 3), pl.ds(pl.multiple_of(row, 16), count)]
-        return remote(at, at, send, recv, i, near[name])
-
-    def tiny(i, sec, name):
+    made = []
+
+    def go(sec, slot, row, count, name):
+        at = w_ref.at[core, sec * 3 + slot, pl.ds(pl.multiple_of(row, 16), count)]
+        c = remote(at, at, send, recv, len(made), near[name])
+        made.append(c)
+        c.start()
+        return c
+
+    def tiny(sec, name):
         at = s_ref.at[pl.ds(sec * 3, 3)]
-        return remote(at, at, send, recv, i, near[name])
+        c = remote(at, at, send, recv, len(made), near[name])
+        made.append(c)
+        c.start()
+        return c
 
     mine, other = 128 * (2 * zp + xl), 128 * (2 * zp + 1 - xl)
-    t = {
-        0: piece(0, own, 256 * zp, 256, "y"),
-        1: piece(1, own, other, 128, "xd"),
-        2: piece(2, sec_x, mine, 128, "xs"),
-        3: piece(3, sec_x, mine, 64, "z+"),
-        4: piece(4, sec_x, mine + 64, 64, "z-"),
-        5: piece(5, sec_y, other, 128, "xd"),
-        6: piece(6, sec_y, 256 * zp, 128, "z+"),
-        7: piece(7, sec_y, 256 * zp + 128, 128, "z-"),
-        8: piece(8, sec_xy, mine, 128, "xs"),
-        9: piece(9, sec_xy, mine, 64, "z+"),
-        10: piece(10, sec_xy, mine + 64, 64, "z-"),
-        11: piece(11, sec_x, other, 64, "z+"),
-        12: piece(12, sec_x, other + 64, 64, "z-"),
-        13: piece(13, sec_xy, other, 64, "z+"),
-        14: piece(14, sec_xy, other + 64, 64, "z-"),
-        15: piece(15, sec_y, 256 * zp, 256, "core"),
-        16: piece(16, sec_y, 256 * (1 - zp), 256, "core"),
-        17: piece(17, sec_x, 256 * zp, 256, "core"),
-        18: piece(18, sec_x, 256 * (1 - zp), 256, "core"),
-        19: piece(19, sec_xy, 256 * zp, 256, "core"),
-        20: piece(20, sec_xy, 256 * (1 - zp), 256, "core"),
-        21: tiny(21, own, "y"),
-        22: tiny(22, own, "xd"),
-        23: tiny(23, sec_y, "xd"),
-    }
-
-    def go(*ids):
-        for i in ids:
-            t[i].start()
-
-    def got(*ids):
-        for i in ids:
-            t[i].wait_recv()
-
-    go(21, 22, 1, 0)
-    got(21)
-    go(23)
-    got(1)
-    go(2, 3, 4)
-    got(0)
-    go(5, 6, 7, 15)
-    got(2)
-    go(11, 12, 17)
-    got(5)
-    go(8, 9, 10)
-    got(6, 7)
-    go(16)
-    got(8)
-    go(13, 14, 19)
-    got(3, 4, 11, 12)
-    go(18)
-    got(9, 10, 13, 14)
-    go(20)
-    got(22, 23, 15, 16, 17, 18, 19, 20)
-    for i in range(24):
-        t[i].wait_send()
+
+    def to_z(sec, slot, row):
+        return [go(sec, slot, row, 64, "z+"), go(sec, slot, row + 64, 64, "z-")]
+
+    t_y, t_x = tiny(own, "y"), tiny(own, "xd")
+    x1, ya, yb, x2, xy1, xy2, zx, zy, zxy, twin = [], [], [], [], [], [], [], [], [], []
+    for s in range(3):
+        x1.append(go(own, s, other, 128, "xd"))
+        ya.append(go(own, s, other, 128, "y"))
+    for s in range(3):
+        yb.append(go(own, s, mine, 128, "y"))
+    t_y.wait_recv()
+    t_xy = tiny(sec_y, "xd")
+    for s in range(3):
+        x1[s].wait_recv()
+        x2.append(go(sec_x, s, mine, 128, "xs"))
+        zx.append(to_z(sec_x, s, mine))
+        ya[s].wait_recv()
+        xy1.append(go(sec_y, s, other, 128, "xd"))
+        zy.append(to_z(sec_y, s, other))
+    for s in range(3):
+        x2[s].wait_recv()
+        zx[s] += to_z(sec_x, s, other)
+        twin.append(go(sec_x, s, 256 * zp, 256, "core"))
+    for s in range(3):
+        xy1[s].wait_recv()
+        xy2.append(go(sec_xy, s, mine, 128, "xs"))
+        zxy.append(to_z(sec_xy, s, mine))
+        yb[s].wait_recv()
+        zy[s] += to_z(sec_y, s, mine)
+        twin.append(go(sec_y, s, 256 * zp, 256, "core"))
+    for s in range(3):
+        xy2[s].wait_recv()
+        zxy[s] += to_z(sec_xy, s, other)
+        twin.append(go(sec_xy, s, 256 * zp, 256, "core"))
+    for sec, group in ((sec_x, zx), (sec_y, zy), (sec_xy, zxy)):
+        for s in range(3):
+            for c in group[s]:
+                c.wait_recv()
+            twin.append(go(sec, s, 256 * (1 - zp), 256, "core"))
+    for c in twin + [t_x, t_xy]:
+        c.wait_recv()
+    for c in made:
+        c.wait_send()
 
 
 def gather(w_mix, w_point, small):
@@ -151,13 +146,13 @@
             jax.ShapeDtypeStruct((CELLS, 16, CH), BF),
         ),
         in_specs=[pl.BlockSpec(memory_space=pl.ANY)] * 3,
-        out_specs=(pl.BlockSpec(memory_space=pl.ANY),) * 2,
+        out_specs=(pl.BlockSpec(memory_space=pltpu.VMEM),) * 2,
         scratch_shapes=[
-            pltpu.SemaphoreType.DMA((24,)),
-            pltpu.SemaphoreType.DMA((24,)),
+            pltpu.SemaphoreType.DMA((75,)),
+            pltpu.SemaphoreType.DMA((75,)),
             pltpu.SemaphoreType.DMA((3,)),
         ],
-        compiler_params=pltpu.CompilerParams(collective_id=1, has_side_effects=True),
+        compiler_params=pltpu.CompilerParams(collective_id=1, has_side_effects=True, vmem_limit_bytes=40 << 20),
         name="gather",
     )(w_mix, w_point, small)
 
@@ -281,7 +276,7 @@
             scratch_shapes=[pltpu.VMEM((ROWS, CH), BF)],
         ),
         out_shape=out_shape,
-        compiler_params=pltpu.CompilerParams(vmem_limit_bytes=32 << 20),
+        compiler_params=pltpu.CompilerParams(vmem_limit_bytes=56 << 20),
         name="forward_save" if save else "forward",
     )(*args)
 
@@ -292,9 +287,9 @@
 
 def bwd_kernel(wgrad, flags, ga_ref, gb_ref, w_ref, k_ref, sp_ref, so_ref, ss_ref, st_ref, *rest):
     if wgrad:
-        gw_ref, gk_ref, o_ref, gs = rest
+        gw_ref, gk_ref, o_ref, gs, taps = rest
     else:
-        o_ref, gs = rest
+        o_ref, gs, taps = rest
     i = pl.program_id(0)
     cell = CELLS - 1 - i
 
@@ -335,10 +330,11 @@
             if wgrad:
                 a = jnp.maximum(older.astype(F32), 0.0)
                 for v in range(3):
-                    gk_ref[0, v : v + 1, cols] = jnp.sum(a[:-PITCH] * gv[v][PITCH:], axis=0, keepdims=True)
-                    gk_ref[0, 3 + v : 4 + v, cols] = jnp.sum(a * gv[v], axis=0, keepdims=True)
-                    gk_ref[0, 6 + v : 7 + v, cols] = jnp.sum(a[PITCH:] * gv[v][:-PITCH], axis=0, keepdims=True)
+                    taps[v : v + 1, cols] = jnp.sum(a[:-PITCH] * gv[v][PITCH:], axis=0, keepdims=True)
+                    taps[3 + v : 4 + v, cols] = jnp.sum(a * gv[v], axis=0, keepdims=True)
+                    taps[6 + v : 7 + v, cols] = jnp.sum(a[PITCH:] * gv[v][:-PITCH], axis=0, keepdims=True)
         if wgrad:
+            gk_ref[0] = taps[...].astype(BF)
             gw_ref[0, 0] = lax.dot_general(jnp.maximum(prev, 0), gh, TN, preferred_element_type=F32).astype(BF)
             gw_ref[1, 0] = lax.dot_general(ss_ref[0], gh, TN, preferred_element_type=F32).astype(BF)
 
@@ -359,7 +355,7 @@
         out_specs = [both, one((16, CH))] + out_specs
         out_shape = [
             jax.ShapeDtypeStruct((2, CELLS, CH, CH), BF),
-            jax.ShapeDtypeStruct((CELLS, 16, CH), F32),
+            jax.ShapeDtypeStruct((CELLS, 16, CH), BF),
         ] + out_shape
     return pl.pallas_call(
         functools.partial(bwd_kernel, wgrad),
@@ -368,15 +364,15 @@
             grid=(CELLS,),
             in_specs=[whole((2, ROWS, CH)), whole((2, ROWS, CH)), both, one((16, CH))] + [one((ROWS, CH))] * 4,
             out_specs=out_specs,
-            scratch_shapes=[pltpu.VMEM((ROWS, CH), F32)],
+            scratch_shapes=[pltpu.VMEM((ROWS, CH), F32), pltpu.VMEM((16, CH), F32)],
         ),
         out_shape=out_shape,
-        compiler_params=pltpu.CompilerParams(vmem_limit_bytes=32 << 20),
+        compiler_params=pltpu.CompilerParams(vmem_limit_bytes=56 << 20),
         name="backward_weights" if wgrad else "backward",
     )(flags, arrived, head, weights, small, *saved)
 
 
-def sum_kernel(g_ref, o_ref, acc, rb, zp0, zp, xp0, xp, ap0, ap, bp0, bp, yb, ob, send, recv, local):
+def sum_kernel(g_ref, k_ref, o_ref, t_ref, tk, tr, ty, tx, tz, acc, rb, zp0, zp, xp0, xp, ap0, ap, bp0, bp, yb, ob, send, recv, local):
     _, _, y, xh, z, xl, core = place()
     near = neighbours()
     yl = y % 2
@@ -392,7 +388,11 @@
 
     load = pltpu.make_async_copy(g_ref.at[core], acc, local.at[0])
     load.start()
+    load_taps = pltpu.make_async_copy(k_ref, tk, local.at[1])
+    load_taps.start()
     greet(("core", "xs", "xd", "z+", "z-", "y"), near)
+    load_taps.wait()
+    step = move(tk, tr, "core")
     twin = [move(g_ref.at[1 - core, a, b], rb.at[a, b], "core") for a in range(2) for b in range(2)]
     load.wait()
     for j in range(4):
@@ -448,6 +448,16 @@
 
         lax.fori_loop(0, 4, step, 0)
 
+    def fold(dst, a, b):
+        for s in range(3):
+            dst[s] = (a[s].astype(F32) + b[s].astype(F32)).astype(BF)
+
+    step.wait_recv()
+    for a in range(2):
+        for b in range(2):
+            fold(tr.at[a, b], tr.at[a, b], tk.at[a, b])
+    step = move(tr.at[1 - yl], ty, "y")
+
     za = [move(a1(4).at[:, :, :, 0], zp0.at[0], "z+"), move(a1(4).at[:, :, :, 1], zp0.at[1], "z-")]
     xa = [move(b1(2).at[0], xp0.at[0], "x+"), move(b1(2).at[1], xp0.at[1], "x-")]
 
@@ -456,6 +466,10 @@
     plus4(a1(3).at[:, :, :, 0], zp0.at[0])
     plus4(a1(-3).at[:, :, :, 1], zp0.at[1])
     za = [move(a1(3), zp.at[0, 0], "z+"), move(a1(-3), zp.at[0, 1], "z-")]
+    step.wait_recv()
+    for b in range(2):
+        fold(ty.at[b], ty.at[b], tr.at[yl, b])
+    step = move(ty.at[1 - xh], tx.at[0], "xd")
 
     for c in xa:
         c.wait_recv()
@@ -470,6 +484,10 @@
     plus1(b1(1).at[0], xp0.at[0])
     plus1(b1(-1).at[1], xp0.at[1])
     xa = [move(b1(1), xp.at[0], "x+"), move(b1(-1), xp.at[1], "x-")]
+
+    step.wait_recv()
+    fold(tx.at[0], tx.at[0], ty.at[xh])
+    step = move(tx.at[0], tx.at[1], "xs")
 
     for k in (2, 1):
         for c in za:
@@ -478,6 +496,10 @@
         plus4(a1(-k), zp.at[2 - k, 1])
         za = [move(a1(k), zp.at[3 - k, 0], "z+"), move(a1(-k), zp.at[3 - k, 1], "z-")]
 
+    step.wait_recv()
+    fold(tz.at[0, 0], tx.at[0], tx.at[1])
+    step = [move(tz.at[0, 0], tz.at[1, 0], "z+"), move(tz.at[0, 0], tz.at[1, 1], "z-")]
+
     for c in xa:
         c.wait_recv()
     plus(b1(0), xp.at[0], xp.at[1])
@@ -501,6 +523,9 @@
     xb = [move(a2(1), ap.at[0], "x+"), move(a2(-1), ap.at[1], "x-")]
 
     for k in (2, 1):
+        for c in step:
+            c.wait_recv()
+        step = [move(tz.at[3 - k, 0], tz.at[4 - k, 0], "z+"), move(tz.at[3 - k, 1], tz.at[4 - k, 1], "z-")]
         for c in zb:
             c.wait_recv()
         plus(b2(k), bp.at[2 - k, 0])
@@ -518,6 +543,10 @@
         ya[c].wait_recv()
         for s in range(3):
             ob[core, s, z, c, xl] = (acc[yl, xh, s, z, c, xl].astype(F32) + yb[c, s].astype(F32)).astype(BF)
+
+    for c in step:
+        c.wait_recv()
+    step = move(tz.at[3, 0], tz.at[4, 0], "z+")
 
     def both_cores(at):
         return move(at, at, "core")
@@ -549,19 +578,30 @@
         c.wait_send()
     done = pltpu.make_async_copy(ob, o_ref, local.at[0])
     done.start()
+    step.wait_recv()
+    for s in range(3):
+        v = tz[0, 0, s].astype(F32) + tz[4, 0, s].astype(F32)
+        for k in (1, 2, 3):
+            v = v + tz[k, 0, s].astype(F32) + tz[k, 1, s].astype(F32)
+        t_ref[s] = v
     done.wait()
 
 
-def sum_up(grads):
-    n = 64
+def sum_up(grads, taps):
+    n = 80
     lead = (16, CH)
     shape = lambda *d: pltpu.VMEM(d + lead, BF)
     return pl.pallas_call(
         sum_kernel,
-        out_shape=jax.ShapeDtypeStruct((2, 3, 8, 2, 2, 16, CH), BF),
-        in_specs=[pl.BlockSpec(memory_space=pl.ANY)],
-        out_specs=pl.BlockSpec(memory_space=pl.ANY),
+        out_shape=(jax.ShapeDtypeStruct((2, 3, 8, 2, 2, 16, CH), BF), jax.ShapeDtypeStruct((3, 16, CH), F32)),
+        in_specs=[pl.BlockSpec(memory_space=pl.ANY)] * 2,
+        out_specs=(pl.BlockSpec(memory_space=pl.ANY), pl.BlockSpec(memory_space=pltpu.VMEM)),
         scratch_shapes=[
+            shape(2, 2, 3),
+            shape(2, 2, 3),
+            shape(2, 3),
+            shape(2, 3),
+            shape(5, 2, 3),
             shape(2, 2, 3, 8, 2, 2),
             shape(2, 2, 3, 8, 2, 2),
             shape(2, 2, 2, 3),
@@ -576,11 +616,11 @@
             shape(2, 3, 8, 2, 2),
             pltpu.SemaphoreType.DMA((n,)),
             pltpu.SemaphoreType.DMA((n,)),
-            pltpu.SemaphoreType.DMA((1,)),
+            pltpu.SemaphoreType.DMA((2,)),
         ],
         compiler_params=pltpu.CompilerParams(collective_id=3, has_side_effects=True, vmem_limit_bytes=48 << 20),
         name="sum_up",
-    )(grads)
+    )(grads, taps)
 
 
 def shards(features, labels, classifier, w_mix, w_point, kernels, counts):
@@ -604,15 +644,9 @@
     (back,) = backward(flags, head, head, weights, smalls, saved, False)
     arrived = hop(back)
     grads, kernel_grads, _ = backward(flags, arrived, head, weights, smalls, saved, True)
-    summed = sum_up(grads.reshape(2, 2, 2, 3, 8, 2, 2, 16, CH))
+    summed, taps = sum_up(grads.reshape(2, 2, 2, 3, 8, 2, 2, 16, CH), kernel_grads.reshape(2, 2, 3, 16, CH))
     summed = summed.reshape(2, 3, CH, CH).astype(F32)
-
-    mine = kernel_grads[:, :9]
-    wide = jnp.zeros((2, CELLS, 9, CH), F32)
-    wide = lax.dynamic_update_index_in_dim(wide, mine, stage, 0).reshape(24, 9, CH)
-    wide = lax.psum(wide, ("segment", "dp"))
-    tap = lax.dynamic_slice_in_dim(wide, (y * 2 + xh) * 3, 3, 0)
-    return summed[0], summed[1], tap
+    return summed[0], summed[1], taps[:, :9]
 
 
 def solution(mesh):

time: 525 us -> 265 us (0.50)
  waiting for transfers between devices: 142 us -> 0 us
  Pallas kernels: 333 us -> 245 us
  local copies, waits for them, and re-layouts: 32.4 us -> 12.9 us
  between operations: 15 us -> 1.49 us
    psum x1 -> x0, waiting for transfers between devices: 142 us -> none  [shards(): wide = lax.psum(wide, ('segment', 'dp'))]
    pallas_call x1, Pallas kernels: 152 us -> 49.8 us  [gather(): pl.pallas_call(gather_kernel, out_shape=(jax.ShapeDtypeStruct((2, CELLS,...]
    unnamed x39 -> x12, local copies, waits for them, and re-layouts: 22.9 us -> 5.2 us
    pallas_call x2, Pallas kernels: 22.5 us -> 28.1 us  [forward(): pl.pallas_call(functools.partial(fwd_kernel, save), grid_spec=pltpu.Prefe...]
  transfers between devices with their start and end apart: 1 -> 0, of which waited for: 1 -> 0; matrix products, arithmetic and copies ran while one was open for 1% -> 0% of each run, Pallas kernels for 19% -> 0%
where the time goes in v2:
time: 265 us; the launch traced here: 261 us
  Pallas kernels  245 us (92%)
  local copies, waits for them, and re-layouts  12.9 us (5%)
    pallas_call x1, Pallas kernels, sum_up(): pl.pallas_call(sum_kernel, out_shape=(jax.ShapeDtypeStruct((2, 3, 8, 2, 2...  100 us
    pallas_call x1, Pallas kernels, gather(): pl.pallas_call(gather_kernel, out_shape=(jax.ShapeDtypeStruct((2, CELLS,...  49.8 us
    pallas_call x2, Pallas kernels, backward(): pl.pallas_call(functools.partial(bwd_kernel, wgrad), grid_spec=pltpu.Pref...  39.2 us
    pallas_call x2, Pallas kernels, forward(): pl.pallas_call(functools.partial(fwd_kernel, save), grid_spec=pltpu.Prefe...  28.1 us
    pallas_call x2, Pallas kernels, hop(): pl.pallas_call(hop_kernel, out_shape=jax.ShapeDtypeStruct(x.shape, x.dtyp...  27.9 us

profile of v2, /device:TPU:1, one launch (start us, length us, event | category | flops | bytes accessed | tf_op | source)
XLA Modules:
  0.0 260.9 jit_solution(13530851395686092132)
XLA Ops:
  0.6 0.0 copy-start
  1.4 1.3 dynamic_slice.8
  2.7 1.3 pad.11.rest_0_
  4.0 0.8 copy.12
  4.8 0.0 copy-done
  4.9 0.7 pad.10
  5.6 0.0 copy-start.2
  5.6 1.4 copy-done.2
  7.0 0.0 copy-start.3
  7.0 1.4 copy-done.3
  8.4 49.8 %gather.1 = (bf16[2,12,512,512]{3,2,1,0:T(8,128)(2,1)}, bf16[12,16,512]{2,1,0:T(8,128)(2,1)S(1)}) custom-call(bf16[3,512,512]{2,1,0:T(8,128)(2,1)S(1)} %copy-done.2, bf16[3,512,512]{2,1,0:T(8,128)(2,1)S(1)} %copy-done.3, bf16[3,16,512]{2,1,0:T(8,128)(2,1)S(1)} %concatenate.9.small_ref), custom_call_target="tpu_custom_call" | custom-call | tf_op jit(solution)/shard_map/gather/pallas_call | solution.py:142
  58.2 0.0 copy-start.1
  58.2 0.2 convert_reduce_fusion
  58.4 1.3 fusion.2
  59.7 0.8 broadcast_in_dim.4.xb_ref
  60.5 0.0 copy-done.1
  60.5 12.8 %forward.1.x_ref = bf16[2,192,512]{2,1,0:T(8,128)(2,1)} custom-call(s32[14]{0:T(128)} %get-tuple-element.33.flags, bf16[192,512]{1,0:T(8,128)(2,1)} %bitcast.14, bf16[2,192,512]{2,1,0:T(8,128)(2,1)} %broadcast_in_dim.4.xb_ref, bf16[2,12,512,512]{3,2,1,0:T(8,128)(2,1)} %get-tuple-element.15.w_ref, bf16[12,16,512]{2,1,0:T(8,128)(2,1)} %copy-done.1), custom_call_target="tpu_custom_call" | custom-call | tf_op jit(solution)/shard_map/forward/pallas_call | solution.py:269
  73.3 13.2 %hop.2.xb_ref = bf16[2,192,512]{2,1,0:T(8,128)(2,1)} custom-call(bf16[2,192,512]{2,1,0:T(8,128)(2,1)} %forward.1.x_ref), custom_call_target="tpu_custom_call" | custom-call | tf_op jit(solution)/shard_map/hop/pallas_call | solution.py:171
  86.5 15.3 %forward_save.1 = (bf16[2,192,512]{2,1,0:T(8,128)(2,1)}, bf16[12,192,512]{2,1,0:T(8,128)(2,1)}, bf16[12,192,512]{2,1,0:T(8,128)(2,1)}, bf16[12,192,512]{2,1,0:T(...) custom-call(s32[14]{0:T(128)} %get-tuple-element.34.flags, bf16[192,512]{1,0:T(8,128)(2,1)} %bitcast.15, ...), custom_call_target="tpu_custom_call" | custom-call | tf_op jit(solution)/shard_map/forward_save/pallas_call | solution.py:269
  101.8 16.9 %backward.1.x_ref = bf16[2,192,512]{2,1,0:T(8,128)(2,1)} custom-call(s32[14]{0:T(128)} %get-tuple-element.34.flags, bf16[2,192,512]{2,1,0:T(8,128)(2,1)} %get-tuple-element.16.ga_ref.gb_ref, bf16[2,192,512]{2,1,0:T(8,128)(2,1)} %get-tuple-element.16.ga_ref.gb_ref, bf16[2,12,512,512]{3,2,1,0:T(8,128)(2,1)} %get-tuple-element.15.w_ref, ...), custom_call_target="tpu_custom_call" | custom-call | tf_op jit(solution)/shard_map/backward/pallas_call | solution.py:360
  118.6 14.7 %hop.3.ga_ref = bf16[2,192,512]{2,1,0:T(8,128)(2,1)} custom-call(bf16[2,192,512]{2,1,0:T(8,128)(2,1)} %backward.1.x_ref), custom_call_target="tpu_custom_call" | custom-call | tf_op jit(solution)/shard_map/hop/pallas_call | solution.py:171
  133.3 22.3 %backward_weights.1 = (bf16[2,12,512,512]{3,2,1,0:T(8,128)(2,1)}, bf16[12,16,512]{2,1,0:T(8,128)(2,1)}, bf16[2,192,512]{2,1,0:T(8,128)(2,1)}) custom-call(s32[14]{0:T(128)} %get-tuple-element.34.flags, bf16[2,192,512]{2,1,0:T(8,128)(2,1)} %hop.3.ga_ref, bf16[2,192,512]{2,1,0:T(8,128)(2,1)} %get-tuple-element.16.ga_ref.gb_ref, ...), custom_call_target="tpu_custom_call" | custom-call | tf_op jit(solution)/shard_map/backward_weights/pallas_call | solution.py:360
  155.7 0.0 copy-start.4
  155.7 0.9 copy-done.4
  156.6 100.0 %sum_up.1 = (bf16[2,3,8,2,2,16,512]{6,5,4,3,2,1,0:T(8,128)(2,1)S(1)}, f32[3,16,512]{2,1,0:T(8,128)S(1)}) custom-call(bf16[2,2,2,3,8,2,2,16,512]{8,7,6,5,4,3,2,1,0:T(8,128)(2,1)} %bitcast.11, bf16[2,2,3,16,512]{4,3,2,1,0:T(8,128)(2,1)S(1)} %bitcast.9), custom_call_target="tpu_custom_call" | custom-call | tf_op jit(solution)/shard_map/sum_up/pallas_call | solution.py:594
  256.6 0.7 copy.13
  257.3 3.6 %fusion.1 = (f32[1,3,8,2,2,16,512]{6,5,4,3,2,1,0:T(8,128)}, f32[1,3,8,2,2,16,512]{6,5,4,3,2,1,0:T(8,128)}) fusion(bf16[2,3,8,2,2,16,512]{6,5,4,3,2,1,0:T(8,128)(2,1)S(1)} %get-tuple-element.23), kind=kLoop, calls=%fused_computation.6 | loop fusion | bytes 12582912 | tf_op jit(solution)/shard_map/slice | solution.py:649
  (4 shorter events, 0.1 us)
Async XLA Ops:
  0.6 4.1 %copy-start = (bf16[4,144,512]{2,1,0:T(8,128)(2,1)S(1)}, bf16[4,144,512]{2,1,0:T(8,128)(2,1)}, u32[]{:S(2)}) copy-start(bf16[4,144,512]{2,1,0:T(8,128)(2,1)} %param.7) | copy-start | bytes 1769476
  5.6 1.4 copy-start.2
  7.0 1.4 copy-start.3
  58.2 2.3 copy-start.1
  155.7 0.9 copy-start.4

commit v3 on v2

v3 whole, which is shorter than its diff:
```python
import jax
import jax.numpy as jnp
from jax import lax
from jax.experimental import pallas as pl
from jax.experimental.pallas import tpu as pltpu
from jax.sharding import PartitionSpec as P

GRID = 12
PITCH = 16
ROWS = GRID * PITCH
CH = 512
CELLS = 12
EPSILON = 1e-06
MESH = pl.DeviceIdType.MESH
BF = jnp.bfloat16
F32 = jnp.float32


def place():
    seg, dp = lax.axis_index("segment"), lax.axis_index("dp")
    y, xh = seg // 2, seg % 2
    core, xl, z = dp % 2, (dp // 2) % 2, dp // 4
    return seg, dp, y, xh, z, xl, core


def dev(y, xh, z, xl, core):
    return (y * 2 + xh, (z * 2 + xl) * 2 + core)


def neighbours():
    seg, dp, y, xh, z, xl, core = place()
    yp = y + 1 - 2 * (y % 2)
    return {
        "core": dev(y, xh, z, xl, 1 - core),
        "xs": dev(y, xh, z, 1 - xl, core),
        "xd": dev(y, 1 - xh, z, 1 - xl, core),
        "x+": dev(y, jnp.where(xl == 0, xh, 1 - xh), z, 1 - xl, core),
        "x-": dev(y, jnp.where(xl == 1, xh, 1 - xh), z, 1 - xl, core),
        "z+": dev(y, xh, (z + 1) % 8, xl, core),
        "z-": dev(y, xh, (z + 7) % 8, xl, core),
        "y": dev(yp, xh, z, xl, core),
        "hop": dev(3 - y, xh, z, xl, core),
    }


def greet(names, near):
    barrier = pltpu.get_barrier_semaphore()
    for name in names:
        pl.semaphore_signal(barrier, inc=1, device_id=near[name], device_id_type=MESH)
    pl.semaphore_wait(barrier, len(names))


def remote(src, dst, send, recv, i, target):
    return pltpu.make_async_remote_copy(
        src_ref=src, dst_ref=dst, send_sem=send.at[i], recv_sem=recv.at[i], device_id=target, device_id_type=MESH
    )


def down(r):
    return jnp.concatenate([jnp.zeros((PITCH, r.shape[1]), r.dtype), r[:-PITCH]], axis=0)


def up(r):
    return jnp.concatenate([r[PITCH:], jnp.zeros((PITCH, r.shape[1]), r.dtype)], axis=0)


NT = (((1,), (1,)), ((), ()))
TN = (((0,), (0,)), ((), ()))


def parts_of(cell):
    return cell // 6, (cell // 3) % 2, cell % 3


def kernel(
    f_ref, mix_ref, point_ref, small_ref, class_ref, o_ref, t_ref,
    w_ref, s_ref, img, st, ho, hi, sp, so, ss, tt, gs, taps, gw, rb,
    tk, tr, ty, tx, tz, zp0, zp, xp0, xp, ap0, ap, bp0, bp, yb, ob, send, recv, local,
):
    _, _, y, xh, z, xl, core = place()
    near = neighbours()
    stage, yl, zpar = y // 2, y % 2, z % 2
    image = jnp.where(stage == 0, y, 3 - y) * 2 + xh
    own = yl * 2 + xh
    sec_y, sec_x, sec_xy = (1 - yl) * 2 + xh, yl * 2 + (1 - xh), (1 - yl) * 2 + (1 - xh)
    count = [14]
    sends = []

    def move(src, dst, name):
        c = remote(src, dst, send, recv, count[0], near[name])
        count[0] += 1
        sends.append(c)
        c.start()
        return c

    loc = [
        pltpu.make_async_copy(small_ref, s_ref.at[pl.ds(own * 3, 3)], local.at[2]),
        pltpu.make_async_copy(mix_ref, w_ref.at[0, pl.ds(own * 3, 3)], local.at[0]),
        pltpu.make_async_copy(point_ref, w_ref.at[1, pl.ds(own * 3, 3)], local.at[1]),
        pltpu.make_async_copy(f_ref.at[image], img, local.at[3]),
    ]
    for c in loc:
        c.start()
    greet(("core", "xs", "xd", "z+", "z-", "y", "hop"), near)
    for c in loc:
        c.wait()

    def go(sec, slot, row, count, name):
        at = w_ref.at[core, sec * 3 + slot, pl.ds(pl.multiple_of(row, 16), count)]
        return move(at, at, name)

    def tiny(sec, name):
        at = s_ref.at[pl.ds(sec * 3, 3)]
        return move(at, at, name)

    mine, other = 128 * (2 * zpar + xl), 128 * (2 * zpar + 1 - xl)

    def to_z(sec, slot, row):
        return [go(sec, slot, row, 64, "z+"), go(sec, slot, row + 64, 64, "z-")]

    t_y, t_x = tiny(own, "y"), tiny(own, "xd")
    x1, y_first, y_then, x2, xy1, xy2, zx, zy, zxy, twin = [], [], [], [], [], [], [], [], [], []
    for s in range(3):
        x1.append(go(own, s, other, 128, "xd"))
        y_first.append(go(own, s, other, 128, "y"))
    for s in range(3):
        y_then.append(go(own, s, mine, 128, "y"))
    t_y.wait_recv()
    t_xy = tiny(sec_y, "xd")
    for s in range(3):
        x1[s].wait_recv()
        x2.append(go(sec_x, s, mine, 128, "xs"))
        zx.append(to_z(sec_x, s, mine))
        y_first[s].wait_recv()
        xy1.append(go(sec_y, s, other, 128, "xd"))
        zy.append(to_z(sec_y, s, other))
    for s in range(3):
        x2[s].wait_recv()
        zx[s] += to_z(sec_x, s, other)
        twin.append(go(sec_x, s, 256 * zpar, 256, "core"))
    for s in range(3):
        xy1[s].wait_recv()
        xy2.append(go(sec_xy, s, mine, 128, "xs"))
        zxy.append(to_z(sec_xy, s, mine))
        y_then[s].wait_recv()
        zy[s] += to_z(sec_y, s, mine)
        twin.append(go(sec_y, s, 256 * zpar, 256, "core"))
    for s in range(3):
        xy2[s].wait_recv()
        zxy[s] += to_z(sec_xy, s, other)
        twin.append(go(sec_xy, s, 256 * zpar, 256, "core"))
    for sec, group in ((sec_x, zx), (sec_y, zy), (sec_xy, zxy)):
        for s in range(3):
            for c in group[s]:
                c.wait_recv()
            twin.append(go(sec, s, 256 * (1 - zpar), 256, "core"))

    image_in = img[...].astype(F32)
    for r in range(GRID):
        row = jnp.concatenate([image_in[GRID * r : GRID * r + GRID], jnp.zeros((PITCH - GRID, CH), F32)], axis=0)
        st[0, PITCH * r : PITCH * r + PITCH] = row.astype(BF)
        st[1, PITCH * r : PITCH * r + PITCH] = row.astype(BF)
    for c in twin + [t_x, t_xy]:
        c.wait_recv()

    hops = [remote(ho.at[i], hi.at[i], send, recv, 12 + i, near["hop"]) for i in range(2)]
    real = lax.broadcasted_iota(jnp.int32, (ROWS, 128), 0) % PITCH < GRID

    def holds(cell, cols=slice(None)):
        return s_ref[cell, 9:10, cols].astype(F32) > (cell % 3).astype(F32)

    def cell_forward(cell, _):
        sp[cell] = st[0]
        so[cell] = st[1]
        for c in range(4):
            cols = slice(128 * c, 128 * c + 128)
            a = jnp.maximum(st[1, :, cols].astype(F32), 0.0)
            k = s_ref[cell, :, cols].astype(F32)
            am, ap_ = pltpu.roll(a, 1, 0), pltpu.roll(a, ROWS - 1, 0)
            r = [k[3 * u : 3 * u + 1] * am + k[3 * u + 1 : 3 * u + 2] * a + k[3 * u + 2 : 3 * u + 3] * ap_ for u in range(3)]
            s = r[1] + down(r[0]) + up(r[2])
            ss[cell, :, cols] = jnp.where(real, s, 0.0).astype(BF)
        prev = st[0]
        total = jnp.dot(ss[cell], w_ref[1, cell], preferred_element_type=F32)
        total = total + jnp.dot(jnp.maximum(prev, 0), w_ref[0, cell], preferred_element_type=F32)
        prev = prev.astype(F32)
        total = prev + total
        q = lax.rsqrt(jnp.mean(total * total, axis=-1, keepdims=True) + EPSILON)
        tt[cell] = total
        on = holds(cell)
        st[1] = jnp.where(on, prev, st[1].astype(F32)).astype(BF)
        st[0] = jnp.where(on, total * q, prev).astype(BF)
        return 0

    def head():
        last = st[0].astype(F32)
        pooled = jnp.sum(jnp.maximum(last, 0.0), axis=0, keepdims=True) / (GRID * GRID)
        grad = jnp.zeros((1, CH), F32)
        for k in range(4):
            row = class_ref[0, k : k + 1, :]
            logit = jnp.sum(pooled * row, axis=-1, keepdims=True)
            grad = grad + (logit - class_ref[1, k : k + 1, :]) * row
        grad = grad / (GRID * GRID)
        ho[0] = jnp.where(last > 0, jnp.broadcast_to(grad, last.shape), 0.0).astype(BF)
        ho[1] = jnp.zeros((ROWS, CH), BF)

    def twin_of(cell):
        a, b, s = parts_of(cell)
        return remote(gw.at[1 - core, a, b, s], rb.at[a, b, s], send, recv, cell, near["core"])

    def join(cell):
        a, b, s = parts_of(cell)
        twin_of(cell).wait_recv()
        gw[core, a, b, s] = (gw[core, a, b, s].astype(F32) + rb[a, b, s].astype(F32)).astype(BF)

    def cell_backward(i, g, wgrad):
        cell = CELLS - 1 - i
        a_, b_, s_ = parts_of(cell)
        total = tt[cell]
        q = lax.rsqrt(jnp.mean(total * total, axis=-1, keepdims=True) + EPSILON)
        n = total * q
        gn = g[0].astype(F32)
        on = holds(cell)
        gt = q * (gn - n * jnp.mean(gn * n, axis=-1, keepdims=True))
        gt = jnp.where(on, gt, 0.0)
        gh = gt.astype(BF)
        gs[...] = lax.dot_general(gh, w_ref[1, cell], NT, preferred_element_type=F32)
        gm = lax.dot_general(gh, w_ref[0, cell], NT, preferred_element_type=F32)
        prev = sp[cell]
        g[0] = jnp.where(on, gt + jnp.where(prev > 0, gm, 0.0) + g[1].astype(F32), gn).astype(BF)
        for c in range(4):
            cols = slice(128 * c, 128 * c + 128)
            u_ = gs[:, cols]
            k = s_ref[cell, :, cols].astype(F32)
            gv = [pltpu.roll(u_, ROWS - 1, 0), u_, pltpu.roll(u_, 1, 0)]
            r = [
                k[3 * u : 3 * u + 1] * gv[0] + k[3 * u + 1 : 3 * u + 2] * gv[1] + k[3 * u + 2 : 3 * u + 3] * gv[2]
                for u in range(3)
            ]
            rel = r[1] + up(r[0]) + down(r[2])
            older = so[cell, :, cols].astype(F32)
            g[1, :, cols] = jnp.where(holds(cell, cols), jnp.where(older > 0, rel, 0.0), g[1, :, cols].astype(F32)).astype(BF)
            if wgrad:
                a = jnp.maximum(older, 0.0)
                for v in range(3):
                    taps[v : v + 1, cols] = jnp.sum(a[:-PITCH] * gv[v][PITCH:], axis=0, keepdims=True)
                    taps[3 + v : 4 + v, cols] = jnp.sum(a * gv[v], axis=0, keepdims=True)
                    taps[6 + v : 7 + v, cols] = jnp.sum(a[PITCH:] * gv[v][:-PITCH], axis=0, keepdims=True)
        if wgrad:
            tk[a_, b_, s_] = taps[...].astype(BF)
            parts = (8, 2, 2, 16, CH)
            gw[0, a_, b_, s_] = (
                lax.dot_general(jnp.maximum(prev, 0), gh, TN, preferred_element_type=F32).astype(BF).reshape(parts)
            )
            gw[1, a_, b_, s_] = lax.dot_general(ss[cell], gh, TN, preferred_element_type=F32).astype(BF).reshape(parts)
            twin_of(cell).start()

            @pl.when(i >= 2)
            def _():
                join(cell + 2)

        return 0

    taps[...] = jnp.zeros_like(taps)

    @pl.when(stage == 1)
    def _():
        for c in hops:
            c.wait_recv()
        st[...] = hi[...]

    lax.fori_loop(0, CELLS, cell_forward, 0)

    @pl.when(stage == 0)
    def _():
        ho[...] = st[...]
        for c in hops:
            c.start()
        for c in hops:
            c.wait_recv()

    @pl.when(stage == 1)
    def _():
        head()
        hi[...] = ho[...]
        lax.fori_loop(0, CELLS, lambda i, _: cell_backward(i, ho, False), 0)
        for c in hops:
            c.start()

    lax.fori_loop(0, CELLS, lambda i, _: cell_backward(i, hi, True), 0)
    step = move(tk, tr, "core")
    join(jnp.int32(1))
    join(jnp.int32(0))

    acc = gw.at[core]

    def plus(ref, *others):
        def step(s, _):
            v = ref[:, s].astype(F32)
            for o in others:
                v = v + o[:, s].astype(F32)
            ref[:, s] = v.astype(BF)
            return 0

        lax.fori_loop(0, 3, step, 0)

    def zat(d):
        return (z + 8 + d) % 8

    def xat(d):
        x = (xh * 2 + xl + 4 + d) % 4
        return x // 2, x % 2

    def a1(d):
        return acc.at[:, :, :, zat(d), 0]

    def b1(d):
        h, l = xat(d)
        return acc.at[:, h, :, :, 1, l]

    def a2(d):
        h, l = xat(d)
        return acc.at[:, h, :, z, 0, l]

    def b2(d):
        return acc.at[:, xh, :, zat(d), 1, xl]

    def plus4(ref, *others):
        def step(n, _):
            a, b = n // 2, n % 2
            v = ref[a, b].astype(F32)
            for o in others:
                v = v + o[a, b].astype(F32)
            ref[a, b] = v.astype(BF)
            return 0

        lax.fori_loop(0, 4, step, 0)

    def fold(dst, a, b):
        for s in range(3):
            dst[s] = (a[s].astype(F32) + b[s].astype(F32)).astype(BF)

    step.wait_recv()
    for a in range(2):
        for b in range(2):
            fold(tr.at[a, b], tr.at[a, b], tk.at[a, b])
    step = move(tr.at[1 - yl], ty, "y")

    za = [move(a1(4).at[:, :, :, 0], zp0.at[0], "z+"), move(a1(4).at[:, :, :, 1], zp0.at[1], "z-")]
    xa = [move(b1(2).at[0], xp0.at[0], "x+"), move(b1(2).at[1], xp0.at[1], "x-")]

    for c in za:
        c.wait_recv()
    plus4(a1(3).at[:, :, :, 0], zp0.at[0])
    plus4(a1(-3).at[:, :, :, 1], zp0.at[1])
    za = [move(a1(3), zp.at[0, 0], "z+"), move(a1(-3), zp.at[0, 1], "z-")]
    step.wait_recv()
    for b in range(2):
        fold(ty.at[b], ty.at[b], tr.at[yl, b])
    step = move(ty.at[1 - xh], tx.at[0], "xd")

    for c in xa:
        c.wait_recv()

    def plus1(ref, other):
        def step(s, _):
            ref[s] = (ref[s].astype(F32) + other[s].astype(F32)).astype(BF)
            return 0

        lax.fori_loop(0, 3, step, 0)

    plus1(b1(1).at[0], xp0.at[0])
    plus1(b1(-1).at[1], xp0.at[1])
    xa = [move(b1(1), xp.at[0], "x+"), move(b1(-1), xp.at[1], "x-")]

    step.wait_recv()
    fold(tx.at[0], tx.at[0], ty.at[xh])
    step = move(tx.at[0], tx.at[1], "xs")

    for k in (2, 1):
        for c in za:
            c.wait_recv()
        plus4(a1(k), zp.at[2 - k, 0])
        plus4(a1(-k), zp.at[2 - k, 1])
        za = [move(a1(k), zp.at[3 - k, 0], "z+"), move(a1(-k), zp.at[3 - k, 1], "z-")]

    step.wait_recv()
    fold(tz.at[0, 0], tx.at[0], tx.at[1])
    step = [move(tz.at[0, 0], tz.at[1, 0], "z+"), move(tz.at[0, 0], tz.at[1, 1], "z-")]

    for c in xa:
        c.wait_recv()
    plus(b1(0), xp.at[0], xp.at[1])
    zb = [move(b2(4).at[0], bp0.at[0], "z+"), move(b2(4).at[1], bp0.at[1], "z-")]

    for c in za:
        c.wait_recv()
    plus4(a1(0), zp.at[2, 0], zp.at[2, 1])
    xb = [move(a2(2).at[0], ap0.at[0], "x+"), move(a2(2).at[1], ap0.at[1], "x-")]

    for c in zb:
        c.wait_recv()
    plus1(b2(3).at[0], bp0.at[0])
    plus1(b2(-3).at[1], bp0.at[1])
    zb = [move(b2(3), bp.at[0, 0], "z+"), move(b2(-3), bp.at[0, 1], "z-")]

    for c in xb:
        c.wait_recv()
    plus1(a2(1).at[0], ap0.at[0])
    plus1(a2(-1).at[1], ap0.at[1])
    xb = [move(a2(1), ap.at[0], "x+"), move(a2(-1), ap.at[1], "x-")]

    for k in (2, 1):
        for c in step:
            c.wait_recv()
        step = [move(tz.at[3 - k, 0], tz.at[4 - k, 0], "z+"), move(tz.at[3 - k, 1], tz.at[4 - k, 1], "z-")]
        for c in zb:
            c.wait_recv()
        plus(b2(k), bp.at[2 - k, 0])
        plus(b2(-k), bp.at[2 - k, 1])
        zb = [move(b2(k), bp.at[3 - k, 0], "z+"), move(b2(-k), bp.at[3 - k, 1], "z-")]
    for c in xb:
        c.wait_recv()
    plus(a2(0), ap.at[0], ap.at[1])
    ya = [move(acc.at[1 - yl, xh, :, z, 0, xl], yb.at[0], "y")]
    for c in zb:
        c.wait_recv()
    plus(b2(0), bp.at[2, 0], bp.at[2, 1])
    ya.append(move(acc.at[1 - yl, xh, :, z, 1, xl], yb.at[1], "y"))
    for c in range(2):
        ya[c].wait_recv()
        for s in range(3):
            ob[core, s, z, c, xl] = (acc[yl, xh, s, z, c, xl].astype(F32) + yb[c, s].astype(F32)).astype(BF)

    for c in step:
        c.wait_recv()
    step = move(tz.at[3, 0], tz.at[4, 0], "z+")

    def both_cores(at):
        return move(at, at, "core")

    mine = ob.at[core, :, z, :, xl]
    pair = move(mine, mine, "xs")
    pair.wait_recv()
    chunk = lambda d: ob.at[core, :, zat(d)]
    last = [both_cores(chunk(0))]
    out = [move(chunk(0), chunk(0), "z+"), move(chunk(0), chunk(0), "z-")]
    for k in (1, 2):
        for c in out:
            c.wait_recv()
        out = [move(chunk(-k), chunk(-k), "z+"), move(chunk(k), chunk(k), "z-")]
        last += [both_cores(chunk(-k)), both_cores(chunk(k))]
    for c in out:
        c.wait_recv()
    out = [
        move(chunk(-3).at[:, 0], chunk(-3).at[:, 0], "z+"),
        move(chunk(3).at[:, 1], chunk(3).at[:, 1], "z-"),
    ]
    last += [both_cores(chunk(-3)), both_cores(chunk(3))]
    for c in out:
        c.wait_recv()
    last += [both_cores(chunk(4))]
    for c in last:
        c.wait_recv()
    done = pltpu.make_async_copy(ob, o_ref, local.at[0])
    done.start()
    step.wait_recv()
    for s in range(3):
        v = tz[0, 0, s].astype(F32) + tz[4, 0, s].astype(F32)
        for k in (1, 2, 3):
            v = v + tz[k, 0, s].astype(F32) + tz[k, 1, s].astype(F32)
        t_ref[s] = v
    for c in sends:
        c.wait_send()
    for c in hops:
        c.wait_send()

    def sent(cell, _):
        twin_of(cell).wait_send()
        return 0

    lax.fori_loop(0, CELLS, sent, 0)
    done.wait()


def shards(features, labels, classifier, w_mix, w_point, kernels, counts):
    _, _, y, xh, z, xl, core = place()
    image = jnp.where(y // 2 == 0, y, 3 - y) * 2 + xh
    tail = jnp.broadcast_to(counts[0].astype(BF), (3, 7, CH))
    small = jnp.concatenate([kernels, tail], axis=1)
    label = lax.dynamic_index_in_dim(labels, image, 0, keepdims=False)
    hot = jnp.broadcast_to((jnp.arange(4) == label).astype(F32)[:, None], (4, CH))
    classes = jnp.pad(jnp.stack([classifier.T, hot]), ((0, 0), (0, 4), (0, 0)))

    lead = (16, CH)
    shape = lambda *d: pltpu.VMEM(d + lead, BF)
    maps = lambda n, t=BF: pltpu.VMEM((n, ROWS, CH), t)
    n = 180
    summed, taps = pl.pallas_call(
        kernel,
        out_shape=(jax.ShapeDtypeStruct((2, 3, 8, 2, 2, 16, CH), BF), jax.ShapeDtypeStruct((3, 16, CH), F32)),
        in_specs=[pl.BlockSpec(memory_space=pl.ANY)] * 4 + [pl.BlockSpec(memory_space=pltpu.VMEM)],
        out_specs=(pl.BlockSpec(memory_space=pl.ANY), pl.BlockSpec(memory_space=pltpu.VMEM)),
        scratch_shapes=[
            pltpu.VMEM((2, CELLS, CH, CH), BF),
            pltpu.VMEM((CELLS, 16, CH), BF),
            pltpu.VMEM((GRID * GRID, CH), BF),
            maps(2),
            maps(2),
            maps(2),
            maps(CELLS),
            maps(CELLS),
            maps(CELLS),
            maps(CELLS, F32),
            pltpu.VMEM((ROWS, CH), F32),
            pltpu.VMEM((16, CH), F32),
            shape(2, 2, 2, 3, 8, 2, 2),
            shape(2, 2, 3, 8, 2, 2),
            shape(2, 2, 3),
            shape(2, 2, 3),
            shape(2, 3),
            shape(2, 3),
            shape(5, 2, 3),
            shape(2, 2, 2, 3),
            shape(3, 2, 2, 2, 3, 2),
            shape(2, 3, 8),
            shape(2, 2, 3, 8),
            shape(2, 3),
            shape(2, 2, 3),
            shape(2, 3),
            shape(3, 2, 2, 3),
            shape(2, 3),
            shape(2, 3, 8, 2, 2),
            pltpu.SemaphoreType.DMA((n,)),
            pltpu.SemaphoreType.DMA((n,)),
            pltpu.SemaphoreType.DMA((4,)),
        ],
        compiler_params=pltpu.CompilerParams(collective_id=1, has_side_effects=True, vmem_limit_bytes=62 << 20),
        name="step",
    )(features, w_mix, w_point, small, classes)
    summed = summed.reshape(2, 3, CH, CH).astype(F32)
    return summed[0], summed[1], taps[:, :9]


def solution(mesh):
    return jax.shard_map(
        shards,
        mesh=mesh,
        in_specs=(
            P("dp", None, None),
            P("dp"),
            P(),
            P("segment", None, None),
            P("segment", None, None),
            P("segment", None, None),
            P("segment"),
        ),
        out_specs=(P("segment", None, None), P("segment", None, None), P("segment", None, None)),
        check_vma=False,
    )
```

time: 265 us -> 218 us (0.82)
  Pallas kernels: 245 us -> 202 us
  local copies, waits for them, and re-layouts: 12.9 us -> 9.76 us
    pallas_call x8 -> x1, Pallas kernels: 245 us -> 202 us  [shards(): pl.pallas_call(kernel, out_shape=(jax.ShapeDtypeStruct((2, 3, 8, 2, 2, 16...]
    unnamed x12 -> x2, local copies, waits for them, and re-layouts: 5.2 us -> 2.34 us
where the time goes in v3:
time: 218 us; the launch traced here: 215 us
  Pallas kernels  202 us (93%)
  local copies, waits for them, and re-layouts  9.76 us (4%)
    pallas_call x1, Pallas kernels, shards(): pl.pallas_call(kernel, out_shape=(jax.ShapeDtypeStruct((2, 3, 8, 2, 2, 16...  202 us
    slice x1, local copies, waits for them, and re-layouts, shards(): return (summed[0], summed[1], taps[:, :9])  5.47 us

profile of v3, /device:TPU:1, one launch (start us, length us, event | category | flops | bytes accessed | tf_op | source)
XLA Modules:
  0.0 215.1 jit_solution(4093868385393452500)
XLA Ops:
  1.3 1.2 dynamic_slice.4
  2.6 0.6 compare_convert_fusion
  3.2 0.1 stack_broadcast_in_dim.2
  3.3 1.3 select_maximum_fusion.class_ref
  4.6 0.8 copy.10
  5.4 0.6 concatenate.3.small_ref
  6.0 202.0 %step.1 = (bf16[2,3,8,2,2,16,512]{6,5,4,3,2,1,0:T(8,128)(2,1)}, f32[3,16,512]{2,1,0:T(8,128)}) custom-call(bf16[4,144,512]{2,1,0:T(8,128)(2,1)} %f_ref.1, bf16[3,512,512]{2,1,0:T(8,128)(2,1)} %mix_ref.1, bf16[3,512,512]{2,1,0:T(8,128)(2,1)} %point_ref.1, bf16[3,16,512]{2,1,0:T(8,128)(2,1)} %concatenate.3.small_ref, f32[2,8,512]{2,1,0:T(8,128)} %select_maximum_fusion.class_ref), custom_call_target="tpu_custom_call" | custom-call | tf_op jit(solution)/shard_map/step/pallas_call | solution.py:499
  208.1 1.6 copy.11
  209.6 5.5 %fusion = (f32[1,3,8,2,2,16,512]{6,5,4,3,2,1,0:T(8,128)}, f32[1,3,8,2,2,16,512]{6,5,4,3,2,1,0:T(8,128)}) fusion(bf16[2,3,8,2,2,16,512]{6,5,4,3,2,1,0:T(8,128)(2,1)} %get-tuple-element.5), kind=kLoop, calls=%fused_computation.3 | loop fusion | bytes 12582912 | tf_op jit(solution)/shard_map/slice | solution.py:542

commit v4 on v3

--- a/solution.py
+++ b/solution.py
@@ -73,8 +73,8 @@
 
 
 def kernel(
-    f_ref, mix_ref, point_ref, small_ref, class_ref, o_ref, t_ref,
-    w_ref, s_ref, img, st, ho, hi, sp, so, ss, tt, gs, taps, gw, rb,
+    f_ref, mix_ref, point_ref, small_ref, class_ref, label_ref, o_ref, t_ref,
+    w_ref, s_ref, img, st, gb, ho, hi, sp, so, ss, tt, gs, taps, gw, rb,
     tk, tr, ty, tx, tz, zp0, zp, xp0, xp, ap0, ap, bp0, bp, yb, ob, send, recv, local,
 ):
     _, _, y, xh, z, xl, core = place()
@@ -92,6 +92,15 @@
         sends.append(c)
         c.start()
         return c
+
+    def spread(pixels, dst, i):
+        for r in range(GRID):
+            row = jnp.concatenate([pixels[GRID * r : GRID * r + GRID], jnp.zeros((PITCH - GRID, CH), F32)], axis=0)
+            dst[i, PITCH * r : PITCH * r + PITCH] = row.astype(BF)
+
+    def packed(maps, i):
+        pixels = maps[i].astype(F32)
+        return jnp.concatenate([pixels[PITCH * r : PITCH * r + GRID] for r in range(GRID)], axis=0).astype(BF)
 
     loc = [
         pltpu.make_async_copy(small_ref, s_ref.at[pl.ds(own * 3, 3)], local.at[2]),
@@ -156,10 +165,8 @@
             twin.append(go(sec, s, 256 * (1 - zpar), 256, "core"))
 
     image_in = img[...].astype(F32)
-    for r in range(GRID):
-        row = jnp.concatenate([image_in[GRID * r : GRID * r + GRID], jnp.zeros((PITCH - GRID, CH), F32)], axis=0)
-        st[0, PITCH * r : PITCH * r + PITCH] = row.astype(BF)
-        st[1, PITCH * r : PITCH * r + PITCH] = row.astype(BF)
+    spread(image_in, st, 0)
+    spread(image_in, st, 1)
     for c in twin + [t_x, t_xy]:
         c.wait_recv()
 
@@ -195,14 +202,16 @@
     def head():
         last = st[0].astype(F32)
         pooled = jnp.sum(jnp.maximum(last, 0.0), axis=0, keepdims=True) / (GRID * GRID)
-        grad = jnp.zeros((1, CH), F32)
-        for k in range(4):
-            row = class_ref[0, k : k + 1, :]
-            logit = jnp.sum(pooled * row, axis=-1, keepdims=True)
-            grad = grad + (logit - class_ref[1, k : k + 1, :]) * row
-        grad = grad / (GRID * GRID)
-        ho[0] = jnp.where(last > 0, jnp.broadcast_to(grad, last.shape), 0.0).astype(BF)
-        ho[1] = jnp.zeros((ROWS, CH), BF)
+        pooled = jnp.broadcast_to(pooled, (8, CH))
+        classes = class_ref[...]
+        logits = lax.dot_general(pooled, classes, NT, precision=lax.Precision.HIGHEST, preferred_element_type=F32)
+        label = label_ref[image].astype(F32)
+        away = jnp.abs(lax.broadcasted_iota(jnp.int32, logits.shape, 1).astype(F32) - label)
+        miss = logits - jnp.maximum(1.0 - away, 0.0)
+        grad = jnp.dot(miss, classes, precision=lax.Precision.HIGHEST, preferred_element_type=F32)
+        grad = grad[:1] / (GRID * GRID)
+        st[0] = jnp.where(last > 0, jnp.broadcast_to(grad, last.shape), 0.0).astype(BF)
+        st[1] = jnp.zeros((ROWS, CH), BF)
 
     def twin_of(cell):
         a, b, s = parts_of(cell)
@@ -255,11 +264,167 @@
             gw[1, a_, b_, s_] = lax.dot_general(ss[cell], gh, TN, preferred_element_type=F32).astype(BF).reshape(parts)
             twin_of(cell).start()
 
-            @pl.when(i >= 2)
+            @pl.when(i >= 1)
             def _():
-                join(cell + 2)
+                join(cell + 1)
+
+            for at, steps in during.items():
+
+                @pl.when(i == at)
+                def _(steps=steps):
+                    for way, group, s, k in steps:
+                        way(group, s, k)
 
         return 0
+
+    acc = gw.at[core]
+    table = {}
+
+    def define(key, make):
+        table[key] = (make, count[0])
+        count[0] += 1
+
+    def copy(key):
+        make, index = table[key]
+        source, target, name = make()
+        return remote(source, target, send, recv, index, near[name])
+
+    def start(*keys):
+        for key in keys:
+            copy(key).start()
+
+    def wait(*keys):
+        for key in keys:
+            copy(key).wait_recv()
+
+    def zat(d):
+        return (z + 8 + d) % 8
+
+    def xat(d):
+        x = (xh * 2 + xl + 4 + d) % 4
+        return x // 2, x % 2
+
+    def a1(g, s, d):
+        return acc.at[g, :, s, zat(d), 0]
+
+    def b1(g, s, d):
+        h, l = xat(d)
+        return acc.at[g, h, s, :, 1, l]
+
+    def a2(g, d):
+        h, l = xat(d)
+        return acc.at[g, h, :, z, 0, l]
+
+    def b2(g, d):
+        return acc.at[g, xh, :, zat(d), 1, xl]
+
+    def plus(ref, *others):
+        v = ref[...].astype(F32)
+        for o in others:
+            v = v + o[...].astype(F32)
+        ref[...] = v.astype(BF)
+
+    SIGN = (1, -1)
+    ZDIR, XDIR = ("z+", "z-"), ("x+", "x-")
+    PART = (pl.ds(0, 2), pl.ds(2, 1))
+    for g in (1, 0):
+        for w in range(2):
+            half = pl.ds(4 * w, 4)
+            for s in range(3):
+                define(("za", g, s, 0, w), lambda g=g, s=s, w=w: (a1(g, s, 4).at[:, w], zp0.at[g, w, s], ZDIR[w]))
+                for k in (1, 2, 3):
+                    define(
+                        ("za", g, s, k, w),
+                        lambda g=g, s=s, w=w, k=k: (a1(g, s, SIGN[w] * (4 - k)), zp.at[g, k - 1, w, s], ZDIR[w]),
+                    )
+                define(
+                    ("xb", g, s, 0, w), lambda g=g, s=s, w=w, half=half: (b1(g, s, 2).at[half], xp0.at[g, w, s], XDIR[w])
+                )
+                define(("xb", g, s, 1, w), lambda g=g, s=s, w=w: (b1(g, s, SIGN[w]), xp.at[g, w, s], XDIR[w]))
+            define(("xa", g, 0, w), lambda g=g, w=w: (a2(g, 2).at[PART[w]], ap0.at[g, PART[w]], XDIR[w]))
+            define(("xa", g, 1, w), lambda g=g, w=w: (a2(g, SIGN[w]), ap.at[g, w], XDIR[w]))
+            define(("zb", g, 0, w), lambda g=g, w=w: (b2(g, 4).at[PART[w]], bp0.at[g, PART[w]], ZDIR[w]))
+            for k in (1, 2, 3):
+                define(("zb", g, k, w), lambda g=g, w=w, k=k: (b2(g, SIGN[w] * (4 - k)), bp.at[g, k - 1, w], ZDIR[w]))
+    for c in range(2):
+        define(("y", c), lambda c=c: (acc.at[1 - yl, xh, :, z, c, xl], yb.at[c], "y"))
+
+    def both(*key):
+        return (*key, 0), (*key, 1)
+
+    def ring_z(g, s, k):
+        if k == 1:
+            start(*both("za", g, s, 0))
+        else:
+            wait(*both("za", g, s, k - 2))
+            for w in range(2):
+                if k == 2:
+                    plus(a1(g, s, SIGN[w] * 3).at[:, w], zp0.at[g, w, s])
+                else:
+                    plus(a1(g, s, SIGN[w] * (5 - k)), zp.at[g, k - 3, w, s])
+            start(*both("za", g, s, k - 1))
+
+    def ring_x(g, s, k):
+        if k == 1:
+            start(*both("xb", g, s, 0))
+        else:
+            wait(*both("xb", g, s, 0))
+            for w in range(2):
+                plus(b1(g, s, SIGN[w]).at[pl.ds(4 * w, 4)], xp0.at[g, w, s])
+            start(*both("xb", g, s, 1))
+
+    def along_z(g, k):
+        if k == 5:
+            for s in range(3):
+                wait(*both("za", g, s, 3))
+                plus(a1(g, s, 0), zp.at[g, 2, 0, s], zp.at[g, 2, 1, s])
+            start(*both("xa", g, 0))
+        elif k == 6:
+            wait(*both("xa", g, 0))
+            for w in range(2):
+                plus(a2(g, SIGN[w]).at[PART[w]], ap0.at[g, PART[w]])
+            start(*both("xa", g, 1))
+        else:
+            wait(*both("xa", g, 1))
+            plus(a2(g, 0), ap.at[g, 0], ap.at[g, 1])
+
+            @pl.when(yl != g)
+            def _():
+                start(("y", 0))
+
+    def along_x(g, k):
+        if k == 3:
+            for s in range(3):
+                wait(*both("xb", g, s, 1))
+                plus(b1(g, s, 0), xp.at[g, 0, s], xp.at[g, 1, s])
+            start(*both("zb", g, 0))
+        elif k <= 6:
+            wait(*both("zb", g, k - 4))
+            for w in range(2):
+                if k == 4:
+                    plus(b2(g, SIGN[w] * 3).at[PART[w]], bp0.at[g, PART[w]])
+                else:
+                    plus(b2(g, SIGN[w] * (7 - k)), bp.at[g, k - 5, w])
+            start(*both("zb", g, k - 3))
+        else:
+            wait(*both("zb", g, 3))
+            plus(b2(g, 0), bp.at[g, 2, 0], bp.at[g, 2, 1])
+
+            @pl.when(yl != g)
+            def _():
+                start(("y", 1))
+
+    z_, x_ = ring_z, ring_x
+    during = {
+        4: [(z_, 1, 2, 1), (x_, 1, 2, 1)],
+        5: [(z_, 1, 1, 1), (x_, 1, 1, 1)],
+        6: [(z_, 1, 0, 1), (x_, 1, 0, 1), (z_, 1, 2, 2)],
+        7: [(z_, 1, 1, 2), (x_, 1, 2, 2)],
+        8: [(z_, 1, 0, 2), (z_, 1, 2, 3), (x_, 1, 1, 2)],
+        9: [(z_, 1, 1, 3), (x_, 1, 0, 2)],
+        10: [(z_, 0, 2, 1), (x_, 0, 2, 1), (z_, 1, 0, 3), (z_, 1, 2, 4)],
+        11: [(z_, 0, 1, 1), (x_, 0, 1, 1), (z_, 1, 1, 4)],
+    }
 
     taps[...] = jnp.zeros_like(taps)
 
@@ -267,239 +432,181 @@
     def _():
         for c in hops:
             c.wait_recv()
-        st[...] = hi[...]
+        for i in range(2):
+            spread(hi[i].astype(F32), st, i)
 
     lax.fori_loop(0, CELLS, cell_forward, 0)
 
     @pl.when(stage == 0)
     def _():
-        ho[...] = st[...]
-        for c in hops:
-            c.start()
-        for c in hops:
-            c.wait_recv()
+        for i in range(2):
+            ho[i] = packed(st, i)
+            hops[i].start()
+        for i in range(2):
+            hops[i].wait_recv()
+            spread(hi[i].astype(F32), gb, i)
 
     @pl.when(stage == 1)
     def _():
         head()
-        hi[...] = ho[...]
-        lax.fori_loop(0, CELLS, lambda i, _: cell_backward(i, ho, False), 0)
-        for c in hops:
-            c.start()
-
-    lax.fori_loop(0, CELLS, lambda i, _: cell_backward(i, hi, True), 0)
+        gb[...] = st[...]
+        lax.fori_loop(0, CELLS, lambda i, _: cell_backward(i, st, False), 0)
+        for i in range(2):
+            ho[i] = packed(st, i)
+            hops[i].start()
+
+    lax.fori_loop(0, CELLS, lambda i, _: cell_backward(i, gb, True), 0)
+    join(jnp.int32(0))
+    z_(0, 0, 1)
+    x_(0, 0, 1)
     step = move(tk, tr, "core")
-    join(jnp.int32(1))
-    join(jnp.int32(0))
-
-    acc = gw.at[core]
-
-    def plus(ref, *others):
-        def step(s, _):
-            v = ref[:, s].astype(F32)
-            for o in others:
-                v = v + o[:, s].astype(F32)
-            ref[:, s] = v.astype(BF)
-            return 0
-
-        lax.fori_loop(0, 3, step, 0)
-
-    def zat(d):
-        return (z + 8 + d) % 8
-
-    def xat(d):
-        x = (xh * 2 + xl + 4 + d) % 4
-        return x // 2, x % 2
-
-    def a1(d):
-        return acc.at[:, :, :, zat(d), 0]
-
-    def b1(d):
-        h, l = xat(d)
-        return acc.at[:, h, :, :, 1, l]
-
-    def a2(d):
-        h, l = xat(d)
-        return acc.at[:, h, :, z, 0, l]
-
-    def b2(d):
-        return acc.at[:, xh, :, zat(d), 1, xl]
-
-    def plus4(ref, *others):
-        def step(n, _):
-            a, b = n // 2, n % 2
-            v = ref[a, b].astype(F32)
-            for o in others:
-                v = v + o[a, b].astype(F32)
-            ref[a, b] = v.astype(BF)
-            return 0
-
-        lax.fori_loop(0, 4, step, 0)
 
     def fold(dst, a, b):
         for s in range(3):
             dst[s] = (a[s].astype(F32) + b[s].astype(F32)).astype(BF)
 
+    z_(1, 0, 4)
+    z_(0, 2, 2)
+    x_(0, 2, 2)
+    along_x(1, 3)
     step.wait_recv()
     for a in range(2):
         for b in range(2):
             fold(tr.at[a, b], tr.at[a, b], tk.at[a, b])
     step = move(tr.at[1 - yl], ty, "y")
-
-    za = [move(a1(4).at[:, :, :, 0], zp0.at[0], "z+"), move(a1(4).at[:, :, :, 1], zp0.at[1], "z-")]
-    xa = [move(b1(2).at[0], xp0.at[0], "x+"), move(b1(2).at[1], xp0.at[1], "x-")]
-
-    for c in za:
-        c.wait_recv()
-    plus4(a1(3).at[:, :, :, 0], zp0.at[0])
-    plus4(a1(-3).at[:, :, :, 1], zp0.at[1])
-    za = [move(a1(3), zp.at[0, 0], "z+"), move(a1(-3), zp.at[0, 1], "z-")]
+    z_(0, 1, 2)
+    x_(0, 1, 2)
+    along_z(1, 5)
+    z_(0, 0, 2)
+    x_(0, 0, 2)
+    along_x(1, 4)
     step.wait_recv()
     for b in range(2):
         fold(ty.at[b], ty.at[b], tr.at[yl, b])
     step = move(ty.at[1 - xh], tx.at[0], "xd")
-
-    for c in xa:
-        c.wait_recv()
-
-    def plus1(ref, other):
-        def step(s, _):
-            ref[s] = (ref[s].astype(F32) + other[s].astype(F32)).astype(BF)
-            return 0
-
-        lax.fori_loop(0, 3, step, 0)
-
-    plus1(b1(1).at[0], xp0.at[0])
-    plus1(b1(-1).at[1], xp0.at[1])
-    xa = [move(b1(1), xp.at[0], "x+"), move(b1(-1), xp.at[1], "x-")]
-
+    z_(0, 2, 3)
+    along_z(1, 6)
+    z_(0, 1, 3)
+    along_x(1, 5)
+    z_(0, 0, 3)
     step.wait_recv()
     fold(tx.at[0], tx.at[0], ty.at[xh])
     step = move(tx.at[0], tx.at[1], "xs")
-
-    for k in (2, 1):
-        for c in za:
-            c.wait_recv()
-        plus4(a1(k), zp.at[2 - k, 0])
-        plus4(a1(-k), zp.at[2 - k, 1])
-        za = [move(a1(k), zp.at[3 - k, 0], "z+"), move(a1(-k), zp.at[3 - k, 1], "z-")]
-
+    along_x(0, 3)
+    along_z(1, 7)
+    z_(0, 2, 4)
+    along_x(1, 6)
+    z_(0, 1, 4)
+    along_x(0, 4)
+    z_(0, 0, 4)
+    along_x(1, 7)
     step.wait_recv()
     fold(tz.at[0, 0], tx.at[0], tx.at[1])
     step = [move(tz.at[0, 0], tz.at[1, 0], "z+"), move(tz.at[0, 0], tz.at[1, 1], "z-")]
-
-    for c in xa:
+    along_x(0, 5)
+    along_z(0, 5)
+    for c in step:
         c.wait_recv()
-    plus(b1(0), xp.at[0], xp.at[1])
-    zb = [move(b2(4).at[0], bp0.at[0], "z+"), move(b2(4).at[1], bp0.at[1], "z-")]
-
-    for c in za:
-        c.wait_recv()
-    plus4(a1(0), zp.at[2, 0], zp.at[2, 1])
-    xb = [move(a2(2).at[0], ap0.at[0], "x+"), move(a2(2).at[1], ap0.at[1], "x-")]
-
-    for c in zb:
-        c.wait_recv()
-    plus1(b2(3).at[0], bp0.at[0])
-    plus1(b2(-3).at[1], bp0.at[1])
-    zb = [move(b2(3), bp.at[0, 0], "z+"), move(b2(-3), bp.at[0, 1], "z-")]
-
-    for c in xb:
-        c.wait_recv()
-    plus1(a2(1).at[0], ap0.at[0])
-    plus1(a2(-1).at[1], ap0.at[1])
-    xb = [move(a2(1), ap.at[0], "x+"), move(a2(-1), ap.at[1], "x-")]
-
-    for k in (2, 1):
-        for c in step:
-            c.wait_recv()
-        step = [move(tz.at[3 - k, 0], tz.at[4 - k, 0], "z+"), move(tz.at[3 - k, 1], tz.at[4 - k, 1], "z-")]
-        for c in zb:
-            c.wait_recv()
-        plus(b2(k), bp.at[2 - k, 0])
-        plus(b2(-k), bp.at[2 - k, 1])
-        zb = [move(b2(k), bp.at[3 - k, 0], "z+"), move(b2(-k), bp.at[3 - k, 1], "z-")]
-    for c in xb:
-        c.wait_recv()
-    plus(a2(0), ap.at[0], ap.at[1])
-    ya = [move(acc.at[1 - yl, xh, :, z, 0, xl], yb.at[0], "y")]
-    for c in zb:
-        c.wait_recv()
-    plus(b2(0), bp.at[2, 0], bp.at[2, 1])
-    ya.append(move(acc.at[1 - yl, xh, :, z, 1, xl], yb.at[1], "y"))
-    for c in range(2):
-        ya[c].wait_recv()
+    step = [move(tz.at[1, 0], tz.at[2, 0], "z+"), move(tz.at[1, 1], tz.at[2, 1], "z-")]
+    along_x(0, 6)
+    along_z(0, 6)
+    along_z(0, 7)
+
+    def landed(c):
+        wait(("y", c))
         for s in range(3):
             ob[core, s, z, c, xl] = (acc[yl, xh, s, z, c, xl].astype(F32) + yb[c, s].astype(F32)).astype(BF)
 
-    for c in step:
+    last = []
+
+    def to(at, name):
+        return move(at, at, name)
+
+    def to_twin(at):
+        last.append(to(at, "core"))
+
+    def chunk(d):
+        return ob.at[core, :, zat(d), 0]
+
+    def piece(d):
+        return ob.at[core, :, zat(d), 1, xl]
+
+    def arrived(copies):
+        for c in copies:
+            c.wait_recv()
+
+    landed(0)
+    pair = to(ob.at[core, :, z, 0, xl], "xs")
+    along_x(0, 7)
+    arrived(step)
+    step = [move(tz.at[2, 0], tz.at[3, 0], "z+"), move(tz.at[2, 1], tz.at[3, 1], "z-")]
+    arrived([pair])
+    out0 = [to(chunk(0), "z+"), to(chunk(0), "z-")]
+    to_twin(chunk(0))
+    landed(1)
+    out1 = [to(piece(0), "z+"), to(piece(0), "z-")]
+    side = [(0, to(piece(0), "xs"))]
+    for k in (1, 2):
+        arrived(out0)
+        out0 = [to(chunk(-k), "z+"), to(chunk(k), "z-")]
+        to_twin(chunk(-k))
+        to_twin(chunk(k))
+        arrived(out1)
+        out1 = [to(piece(-k), "z+"), to(piece(k), "z-")]
+        side += [(-k, to(piece(-k), "xs")), (k, to(piece(k), "xs"))]
+    arrived(out0)
+    out0 = [to(chunk(-3).at[:, 0], "z+"), to(chunk(3).at[:, 1], "z-")]
+    to_twin(chunk(-3))
+    to_twin(chunk(3))
+    arrived(out1)
+    out1 = [to(piece(-3).at[PART[0]], "z+"), to(piece(3).at[PART[1]], "z-")]
+    side += [(-3, to(piece(-3), "xs")), (3, to(piece(3), "xs"))]
+    arrived(step)
+    step = move(tz.at[3, 0], tz.at[4, 0], "z+")
+    arrived(out0)
+    to_twin(chunk(4))
+    arrived(out1)
+    side += [(4, to(piece(4), "xs"))]
+    for d, c in side:
         c.wait_recv()
-    step = move(tz.at[3, 0], tz.at[4, 0], "z+")
-
-    def both_cores(at):
-        return move(at, at, "core")
-
-    mine = ob.at[core, :, z, :, xl]
-    pair = move(mine, mine, "xs")
-    pair.wait_recv()
-    chunk = lambda d: ob.at[core, :, zat(d)]
-    last = [both_cores(chunk(0))]
-    out = [move(chunk(0), chunk(0), "z+"), move(chunk(0), chunk(0), "z-")]
-    for k in (1, 2):
-        for c in out:
-            c.wait_recv()
-        out = [move(chunk(-k), chunk(-k), "z+"), move(chunk(k), chunk(k), "z-")]
-        last += [both_cores(chunk(-k)), both_cores(chunk(k))]
-    for c in out:
-        c.wait_recv()
-    out = [
-        move(chunk(-3).at[:, 0], chunk(-3).at[:, 0], "z+"),
-        move(chunk(3).at[:, 1], chunk(3).at[:, 1], "z-"),
-    ]
-    last += [both_cores(chunk(-3)), both_cores(chunk(3))]
-    for c in out:
-        c.wait_recv()
-    last += [both_cores(chunk(4))]
-    for c in last:
-        c.wait_recv()
-    done = pltpu.make_async_copy(ob, o_ref, local.at[0])
-    done.start()
+        to_twin(ob.at[core, :, zat(d), 1])
     step.wait_recv()
     for s in range(3):
         v = tz[0, 0, s].astype(F32) + tz[4, 0, s].astype(F32)
         for k in (1, 2, 3):
             v = v + tz[k, 0, s].astype(F32) + tz[k, 1, s].astype(F32)
         t_ref[s] = v
+    arrived(last)
+    done = pltpu.make_async_copy(ob, o_ref, local.at[0])
+    done.start()
+    done.wait()
     for c in sends:
         c.wait_send()
     for c in hops:
         c.wait_send()
+    for key in table:
+        copy(key).wait_send()
 
     def sent(cell, _):
         twin_of(cell).wait_send()
         return 0
 
     lax.fori_loop(0, CELLS, sent, 0)
-    done.wait()
 
 
 def shards(features, labels, classifier, w_mix, w_point, kernels, counts):
-    _, _, y, xh, z, xl, core = place()
-    image = jnp.where(y // 2 == 0, y, 3 - y) * 2 + xh
     tail = jnp.broadcast_to(counts[0].astype(BF), (3, 7, CH))
     small = jnp.concatenate([kernels, tail], axis=1)
-    label = lax.dynamic_index_in_dim(labels, image, 0, keepdims=False)
-    hot = jnp.broadcast_to((jnp.arange(4) == label).astype(F32)[:, None], (4, CH))
-    classes = jnp.pad(jnp.stack([classifier.T, hot]), ((0, 0), (0, 4), (0, 0)))
 
     lead = (16, CH)
     shape = lambda *d: pltpu.VMEM(d + lead, BF)
     maps = lambda n, t=BF: pltpu.VMEM((n, ROWS, CH), t)
-    n = 180
+    n = 256
     summed, taps = pl.pallas_call(
         kernel,
         out_shape=(jax.ShapeDtypeStruct((2, 3, 8, 2, 2, 16, CH), BF), jax.ShapeDtypeStruct((3, 16, CH), F32)),
-        in_specs=[pl.BlockSpec(memory_space=pl.ANY)] * 4 + [pl.BlockSpec(memory_space=pltpu.VMEM)],
+        in_specs=[pl.BlockSpec(memory_space=pl.ANY)] * 4
+        + [pl.BlockSpec(memory_space=pltpu.VMEM), pl.BlockSpec(memory_space=pltpu.SMEM)],
         out_specs=(pl.BlockSpec(memory_space=pl.ANY), pl.BlockSpec(memory_space=pltpu.VMEM)),
         scratch_shapes=[
             pltpu.VMEM((2, CELLS, CH, CH), BF),
@@ -507,7 +614,8 @@
             pltpu.VMEM((GRID * GRID, CH), BF),
             maps(2),
             maps(2),
-            maps(2),
+            pltpu.VMEM((2, GRID * GRID, CH), BF),
+            pltpu.VMEM((2, GRID * GRID, CH), BF),
             maps(CELLS),
             maps(CELLS),
             maps(CELLS),
@@ -521,14 +629,14 @@
             shape(2, 3),
             shape(2, 3),
             shape(5, 2, 3),
-            shape(2, 2, 2, 3),
-            shape(3, 2, 2, 2, 3, 2),
-            shape(2, 3, 8),
+            shape(2, 2, 3, 2),
+            shape(2, 3, 2, 3, 2, 2),
+            shape(2, 2, 3, 4),
             shape(2, 2, 3, 8),
             shape(2, 3),
             shape(2, 2, 3),
             shape(2, 3),
-            shape(3, 2, 2, 3),
+            shape(2, 3, 2, 3),
             shape(2, 3),
             shape(2, 3, 8, 2, 2),
             pltpu.SemaphoreType.DMA((n,)),
@@ -537,7 +645,7 @@
         ],
         compiler_params=pltpu.CompilerParams(collective_id=1, has_side_effects=True, vmem_limit_bytes=62 << 20),
         name="step",
-    )(features, w_mix, w_point, small, classes)
+    )(features, w_mix, w_point, small, classifier.T, labels)
     summed = summed.reshape(2, 3, CH, CH).astype(F32)
     return summed[0], summed[1], taps[:, :9]
 

time: 218 us -> 192 us (0.88); the launches traced: 215 us -> 192 us
  Pallas kernels: 202 us -> 182 us
    pallas_call x1, Pallas kernels: 202 us -> 182 us  [shards(): pl.pallas_call(kernel, out_shape=(jax.ShapeDtypeStruct((2, 3, 8, 2, 2, 16...]
where the time goes in v4:
time: 192 us
  Pallas kernels  182 us (95%)
  local copies, waits for them, and re-layouts  8.45 us (4%)
    pallas_call x1, Pallas kernels, shards(): pl.pallas_call(kernel, out_shape=(jax.ShapeDtypeStruct((2, 3, 8, 2, 2, 16...  182 us
    slice x1, local copies, waits for them, and re-layouts, shards(): return (summed[0], summed[1], taps[:, :9])  5.47 us

profile of v4, /device:TPU:1, one launch (start us, length us, event | category | flops | bytes accessed | tf_op | source)
XLA Modules:
  0.0 192.2 jit_solution(17479042381320802029)
XLA Ops:
  1.3 0.8 copy.10
  2.1 0.6 concatenate.3.small_ref
  2.7 182.4 %step.1 = (bf16[2,3,8,2,2,16,512]{6,5,4,3,2,1,0:T(8,128)(2,1)}, f32[3,16,512]{2,1,0:T(8,128)}) custom-call(bf16[4,144,512]{2,1,0:T(8,128)(2,1)} %f_ref.1, bf16[3,512,512]{2,1,0:T(8,128)(2,1)} %mix_ref.1, bf16[3,512,512]{2,1,0:T(8,128)(2,1)} %point_ref.1, bf16[3,16,512]{2,1,0:T(8,128)(2,1)} %concatenate.3.small_ref, f32[4,512]{1,0:T(4,128)} %bitcast.8, ...), custom_call_target="tpu_custom_call" | custom-call | tf_op jit(solution)/shard_map/step/pallas_call | solution.py:605
  185.1 1.6 copy.11
  186.7 5.5 %fusion = (f32[1,3,8,2,2,16,512]{6,5,4,3,2,1,0:T(8,128)}, f32[1,3,8,2,2,16,512]{6,5,4,3,2,1,0:T(8,128)}) fusion(bf16[2,3,8,2,2,16,512]{6,5,4,3,2,1,0:T(8,128)(2,1)} %get-tuple-element.5), kind=kLoop, calls=%fused_computation | loop fusion | bytes 12582912 | tf_op jit(solution)/shard_map/slice | solution.py:650

commit v5 on v4

--- a/solution.py
+++ b/solution.py
@@ -12,6 +12,10 @@
 CELLS = 12
 EPSILON = 1e-06
 MESH = pl.DeviceIdType.MESH
+VMEM_MB = 62
+SEMAPHORES = 300
+Z_LATE = (1, 3, 5, 7)
+X_LATE = 7
 BF = jnp.bfloat16
 F32 = jnp.float32
 
@@ -38,6 +42,8 @@
         "x-": dev(y, jnp.where(xl == 1, xh, 1 - xh), z, 1 - xl, core),
         "z+": dev(y, xh, (z + 1) % 8, xl, core),
         "z-": dev(y, xh, (z + 7) % 8, xl, core),
+        "z4": dev(y, xh, (z + 4) % 8, xl, core),
+        "x2": dev(y, 1 - xh, z, xl, core),
         "y": dev(yp, xh, z, xl, core),
         "hop": dev(3 - y, xh, z, xl, core),
     }
@@ -73,8 +79,8 @@
 
 
 def kernel(
-    f_ref, mix_ref, point_ref, small_ref, class_ref, label_ref, o_ref, t_ref,
-    w_ref, s_ref, img, st, gb, ho, hi, sp, so, ss, tt, gs, taps, gw, rb,
+    f_ref, mix_ref, point_ref, tap_ref, class_ref, label_ref, count_ref, o_ref, t_ref,
+    w_ref, s_ref, img, tin, st, gb, ho, hi, sp, so, ss, tt, gs, taps, gw, rb,
     tk, tr, ty, tx, tz, zp0, zp, xp0, xp, ap0, ap, bp0, bp, yb, ob, send, recv, local,
 ):
     _, _, y, xh, z, xl, core = place()
@@ -103,16 +109,19 @@
         return jnp.concatenate([pixels[PITCH * r : PITCH * r + GRID] for r in range(GRID)], axis=0).astype(BF)
 
     loc = [
-        pltpu.make_async_copy(small_ref, s_ref.at[pl.ds(own * 3, 3)], local.at[2]),
+        pltpu.make_async_copy(tap_ref, tin, local.at[2]),
         pltpu.make_async_copy(mix_ref, w_ref.at[0, pl.ds(own * 3, 3)], local.at[0]),
         pltpu.make_async_copy(point_ref, w_ref.at[1, pl.ds(own * 3, 3)], local.at[1]),
         pltpu.make_async_copy(f_ref.at[image], img, local.at[3]),
     ]
     for c in loc:
         c.start()
-    greet(("core", "xs", "xd", "z+", "z-", "y", "hop"), near)
+    greet(("core", "xs", "xd", "z+", "z-", "z4", "x2", "y", "hop"), near)
     for c in loc:
         c.wait()
+    many = jnp.full((7, CH), count_ref[0].astype(F32), F32)
+    for s in range(3):
+        s_ref[own * 3 + s] = jnp.concatenate([tin[s].astype(F32), many], axis=0).astype(BF)
 
     def go(sec, slot, row, count, name):
         at = w_ref.at[core, sec * 3 + slot, pl.ds(pl.multiple_of(row, 16), count)]
@@ -134,6 +143,7 @@
         y_first.append(go(own, s, other, 128, "y"))
     for s in range(3):
         y_then.append(go(own, s, mine, 128, "y"))
+    y_rest = go(own, 2, 256 * (1 - zpar), 256, "y")
     t_y.wait_recv()
     t_xy = tiny(sec_y, "xd")
     for s in range(3):
@@ -142,7 +152,7 @@
         zx.append(to_z(sec_x, s, mine))
         y_first[s].wait_recv()
         xy1.append(go(sec_y, s, other, 128, "xd"))
-        zy.append(to_z(sec_y, s, other))
+        zy.append(to_z(sec_y, s, other) if s < 2 else [y_rest])
     for s in range(3):
         x2[s].wait_recv()
         zx[s] += to_z(sec_x, s, other)
@@ -152,7 +162,8 @@
         xy2.append(go(sec_xy, s, mine, 128, "xs"))
         zxy.append(to_z(sec_xy, s, mine))
         y_then[s].wait_recv()
-        zy[s] += to_z(sec_y, s, mine)
+        if s < 2:
+            zy[s] += to_z(sec_y, s, mine)
         twin.append(go(sec_y, s, 256 * zpar, 256, "core"))
     for s in range(3):
         xy2[s].wait_recv()
@@ -272,8 +283,8 @@
 
                 @pl.when(i == at)
                 def _(steps=steps):
-                    for way, group, s, k in steps:
-                        way(group, s, k)
+                    for way, *at_step in steps:
+                        way(*at_step)
 
         return 0
 
@@ -304,8 +315,8 @@
         x = (xh * 2 + xl + 4 + d) % 4
         return x // 2, x % 2
 
-    def a1(g, s, d):
-        return acc.at[g, :, s, zat(d), 0]
+    def a1(g, b, s, d):
+        return acc.at[g, b, s, zat(d), 0]
 
     def b1(g, s, d):
         h, l = xat(d)
@@ -323,6 +334,9 @@
         for o in others:
             v = v + o[...].astype(F32)
         ref[...] = v.astype(BF)
+
+    def straight(g, b):
+        return g == 0 and b == 0
 
     SIGN = (1, -1)
     ZDIR, XDIR = ("z+", "z-"), ("x+", "x-")
@@ -331,38 +345,52 @@
         for w in range(2):
             half = pl.ds(4 * w, 4)
             for s in range(3):
-                define(("za", g, s, 0, w), lambda g=g, s=s, w=w: (a1(g, s, 4).at[:, w], zp0.at[g, w, s], ZDIR[w]))
-                for k in (1, 2, 3):
-                    define(
-                        ("za", g, s, k, w),
-                        lambda g=g, s=s, w=w, k=k: (a1(g, s, SIGN[w] * (4 - k)), zp.at[g, k - 1, w, s], ZDIR[w]),
-                    )
+                for b in range(2):
+                    if not straight(g, b):
+                        define(
+                            ("za", g, b, s, 0, w),
+                            lambda g=g, b=b, s=s, w=w: (a1(g, b, s, 4).at[w], zp0.at[g, w, b, s], ZDIR[w]),
+                        )
+                    elif w == 0:
+                        define(("z4", g, b, s), lambda g=g, b=b, s=s: (a1(g, b, s, 4), zp0.at[g, :, b, s], "z4"))
+                    for k in (1, 2, 3):
+                        define(
+                            ("za", g, b, s, k, w),
+                            lambda g=g, b=b, s=s, w=w, k=k: (
+                                a1(g, b, s, SIGN[w] * (4 - k)),
+                                zp.at[g, k - 1, w, b, s],
+                                ZDIR[w],
+                            ),
+                        )
                 define(
                     ("xb", g, s, 0, w), lambda g=g, s=s, w=w, half=half: (b1(g, s, 2).at[half], xp0.at[g, w, s], XDIR[w])
                 )
                 define(("xb", g, s, 1, w), lambda g=g, s=s, w=w: (b1(g, s, SIGN[w]), xp.at[g, w, s], XDIR[w]))
-            define(("xa", g, 0, w), lambda g=g, w=w: (a2(g, 2).at[PART[w]], ap0.at[g, PART[w]], XDIR[w]))
             define(("xa", g, 1, w), lambda g=g, w=w: (a2(g, SIGN[w]), ap.at[g, w], XDIR[w]))
-            define(("zb", g, 0, w), lambda g=g, w=w: (b2(g, 4).at[PART[w]], bp0.at[g, PART[w]], ZDIR[w]))
             for k in (1, 2, 3):
                 define(("zb", g, k, w), lambda g=g, w=w, k=k: (b2(g, SIGN[w] * (4 - k)), bp.at[g, k - 1, w], ZDIR[w]))
+        define(("xa2", g), lambda g=g: (a2(g, 2), ap0.at[g], "x2"))
+        define(("zb4", g), lambda g=g: (b2(g, 4), bp0.at[g], "z4"))
     for c in range(2):
         define(("y", c), lambda c=c: (acc.at[1 - yl, xh, :, z, c, xl], yb.at[c], "y"))
 
     def both(*key):
         return (*key, 0), (*key, 1)
 
-    def ring_z(g, s, k):
-        if k == 1:
-            start(*both("za", g, s, 0))
-        else:
-            wait(*both("za", g, s, k - 2))
+    def ring_z(g, b, s, k):
+        if k == 1 and straight(g, b):
+            start(*both("za", g, b, s, 1))
+            start(("z4", g, b, s))
+        elif k == 1:
+            start(*both("za", g, b, s, 0))
+        elif k > 2 or not straight(g, b):
+            wait(*both("za", g, b, s, k - 2))
             for w in range(2):
                 if k == 2:
-                    plus(a1(g, s, SIGN[w] * 3).at[:, w], zp0.at[g, w, s])
+                    plus(a1(g, b, s, SIGN[w] * 3).at[w], zp0.at[g, w, b, s])
                 else:
-                    plus(a1(g, s, SIGN[w] * (5 - k)), zp.at[g, k - 3, w, s])
-            start(*both("za", g, s, k - 1))
+                    plus(a1(g, b, s, SIGN[w] * (5 - k)), zp.at[g, k - 3, w, b, s])
+            start(*both("za", g, b, s, k - 1))
 
     def ring_x(g, s, k):
         if k == 1:
@@ -376,17 +404,19 @@
     def along_z(g, k):
         if k == 5:
             for s in range(3):
-                wait(*both("za", g, s, 3))
-                plus(a1(g, s, 0), zp.at[g, 2, 0, s], zp.at[g, 2, 1, s])
-            start(*both("xa", g, 0))
-        elif k == 6:
-            wait(*both("xa", g, 0))
-            for w in range(2):
-                plus(a2(g, SIGN[w]).at[PART[w]], ap0.at[g, PART[w]])
+                for b in range(2):
+                    wait(*both("za", g, b, s, 3))
+                    if straight(g, b):
+                        wait(("z4", g, b, s))
+                        plus(a1(g, b, s, 0), zp.at[g, 2, 0, b, s], zp.at[g, 2, 1, b, s], zp0.at[g, :, b, s])
+                    else:
+                        plus(a1(g, b, s, 0), zp.at[g, 2, 0, b, s], zp.at[g, 2, 1, b, s])
             start(*both("xa", g, 1))
+            start(("xa2", g))
         else:
             wait(*both("xa", g, 1))
-            plus(a2(g, 0), ap.at[g, 0], ap.at[g, 1])
+            wait(("xa2", g))
+            plus(a2(g, 0), ap.at[g, 0], ap.at[g, 1], ap0.at[g])
 
             @pl.when(yl != g)
             def _():
@@ -397,34 +427,49 @@
             for s in range(3):
                 wait(*both("xb", g, s, 1))
                 plus(b1(g, s, 0), xp.at[g, 0, s], xp.at[g, 1, s])
-            start(*both("zb", g, 0))
+            start(*both("zb", g, 1))
+            start(("zb4", g))
         elif k <= 6:
             wait(*both("zb", g, k - 4))
             for w in range(2):
-                if k == 4:
-                    plus(b2(g, SIGN[w] * 3).at[PART[w]], bp0.at[g, PART[w]])
-                else:
-                    plus(b2(g, SIGN[w] * (7 - k)), bp.at[g, k - 5, w])
+                plus(b2(g, SIGN[w] * (7 - k)), bp.at[g, k - 5, w])
             start(*both("zb", g, k - 3))
         else:
             wait(*both("zb", g, 3))
-            plus(b2(g, 0), bp.at[g, 2, 0], bp.at[g, 2, 1])
+            wait(("zb4", g))
+            plus(b2(g, 0), bp.at[g, 2, 0], bp.at[g, 2, 1], bp0.at[g])
 
             @pl.when(yl != g)
             def _():
                 start(("y", 1))
 
-    z_, x_ = ring_z, ring_x
-    during = {
-        4: [(z_, 1, 2, 1), (x_, 1, 2, 1)],
-        5: [(z_, 1, 1, 1), (x_, 1, 1, 1)],
-        6: [(z_, 1, 0, 1), (x_, 1, 0, 1), (z_, 1, 2, 2)],
-        7: [(z_, 1, 1, 2), (x_, 1, 2, 2)],
-        8: [(z_, 1, 0, 2), (z_, 1, 2, 3), (x_, 1, 1, 2)],
-        9: [(z_, 1, 1, 3), (x_, 1, 0, 2)],
-        10: [(z_, 0, 2, 1), (x_, 0, 2, 1), (z_, 1, 0, 3), (z_, 1, 2, 4)],
-        11: [(z_, 0, 1, 1), (x_, 0, 1, 1), (z_, 1, 1, 4)],
-    }
+    def z_(n, k):
+        cell = CELLS - 1 - n
+        ring_z(cell // 6, (cell // 3) % 2, cell % 3, k)
+
+    x_ = ring_x
+    during = {at: [] for at in range(1, CELLS)}
+    left = {}
+    for n in range(CELLS):
+        left[n] = []
+        for k, late in enumerate(Z_LATE, 1):
+            if n >= 9 and k == 2:
+                continue
+            if n + late < CELLS:
+                during[n + late].append((z_, n, k))
+            else:
+                left[n].append(k)
+    for at, args in enumerate(((1, 2, 1), (1, 1, 1), (1, 0, 1))):
+        during[4 + at].append((x_, *args))
+    for at, args in enumerate(((1, 2, 2), (1, 1, 2), (1, 0, 2))):
+        during[X_LATE + at].append((x_, *args))
+    during[10].append((x_, 0, 2, 1))
+    during[11].append((x_, 0, 1, 1))
+
+    def z_round():
+        for n in range(CELLS):
+            if left[n]:
+                z_(n, left[n].pop(0))
 
     taps[...] = jnp.zeros_like(taps)
 
@@ -457,7 +502,7 @@
 
     lax.fori_loop(0, CELLS, lambda i, _: cell_backward(i, gb, True), 0)
     join(jnp.int32(0))
-    z_(0, 0, 1)
+    z_(11, left[11].pop(0))
     x_(0, 0, 1)
     step = move(tk, tr, "core")
 
@@ -465,51 +510,42 @@
         for s in range(3):
             dst[s] = (a[s].astype(F32) + b[s].astype(F32)).astype(BF)
 
-    z_(1, 0, 4)
-    z_(0, 2, 2)
+    z_round()
     x_(0, 2, 2)
+    x_(0, 1, 2)
     along_x(1, 3)
     step.wait_recv()
     for a in range(2):
         for b in range(2):
             fold(tr.at[a, b], tr.at[a, b], tk.at[a, b])
     step = move(tr.at[1 - yl], ty, "y")
-    z_(0, 1, 2)
-    x_(0, 1, 2)
-    along_z(1, 5)
-    z_(0, 0, 2)
     x_(0, 0, 2)
-    along_x(1, 4)
+    z_round()
     step.wait_recv()
     for b in range(2):
         fold(ty.at[b], ty.at[b], tr.at[yl, b])
     step = move(ty.at[1 - xh], tx.at[0], "xd")
-    z_(0, 2, 3)
-    along_z(1, 6)
-    z_(0, 1, 3)
     along_x(1, 5)
-    z_(0, 0, 3)
+    z_round()
+    along_z(1, 5)
     step.wait_recv()
     fold(tx.at[0], tx.at[0], ty.at[xh])
     step = move(tx.at[0], tx.at[1], "xs")
     along_x(0, 3)
+    along_x(1, 6)
+    while any(left.values()):
+        z_round()
     along_z(1, 7)
-    z_(0, 2, 4)
-    along_x(1, 6)
-    z_(0, 1, 4)
-    along_x(0, 4)
-    z_(0, 0, 4)
-    along_x(1, 7)
     step.wait_recv()
     fold(tz.at[0, 0], tx.at[0], tx.at[1])
     step = [move(tz.at[0, 0], tz.at[1, 0], "z+"), move(tz.at[0, 0], tz.at[1, 1], "z-")]
     along_x(0, 5)
     along_z(0, 5)
+    along_x(1, 7)
+    along_x(0, 6)
     for c in step:
         c.wait_recv()
     step = [move(tz.at[1, 0], tz.at[2, 0], "z+"), move(tz.at[1, 1], tz.at[2, 1], "z-")]
-    along_x(0, 6)
-    along_z(0, 6)
     along_z(0, 7)
 
     def landed(c):
@@ -525,61 +561,73 @@
     def to_twin(at):
         last.append(to(at, "core"))
 
-    def chunk(d):
-        return ob.at[core, :, zat(d), 0]
-
-    def piece(d):
-        return ob.at[core, :, zat(d), 1, xl]
+    def piece(c, d):
+        return ob.at[core, :, zat(d), c, xl]
 
     def arrived(copies):
         for c in copies:
             c.wait_recv()
 
-    landed(0)
-    pair = to(ob.at[core, :, z, 0, xl], "xs")
+    out = [None, None]
+    side = []
+
+    def beside(c, d):
+        side.append((c, d, to(piece(c, d), "xs")))
+
+    def first(c):
+        landed(c)
+        out[c] = [to(piece(c, 0), "z+"), to(piece(c, 0), "z-")]
+        beside(c, 0)
+
+    def next_one(c, k):
+        arrived(out[c])
+        if k < 3:
+            out[c] = [to(piece(c, -k), "z+"), to(piece(c, k), "z-")]
+        else:
+            out[c] = [to(piece(c, -3).at[PART[0]], "z+"), to(piece(c, 3).at[PART[1]], "z-")]
+        beside(c, -k)
+        beside(c, k)
+
+    def settle(n):
+        for c, d, copy_of in side[:n]:
+            copy_of.wait_recv()
+            last.append(to(ob.at[core, :, zat(d), c], "core"))
+        del side[:n]
+
+    first(0)
     along_x(0, 7)
+    first(1)
     arrived(step)
     step = [move(tz.at[2, 0], tz.at[3, 0], "z+"), move(tz.at[2, 1], tz.at[3, 1], "z-")]
-    arrived([pair])
-    out0 = [to(chunk(0), "z+"), to(chunk(0), "z-")]
-    to_twin(chunk(0))
-    landed(1)
-    out1 = [to(piece(0), "z+"), to(piece(0), "z-")]
-    side = [(0, to(piece(0), "xs"))]
-    for k in (1, 2):
-        arrived(out0)
-        out0 = [to(chunk(-k), "z+"), to(chunk(k), "z-")]
-        to_twin(chunk(-k))
-        to_twin(chunk(k))
-        arrived(out1)
-        out1 = [to(piece(-k), "z+"), to(piece(k), "z-")]
-        side += [(-k, to(piece(-k), "xs")), (k, to(piece(k), "xs"))]
-    arrived(out0)
-    out0 = [to(chunk(-3).at[:, 0], "z+"), to(chunk(3).at[:, 1], "z-")]
-    to_twin(chunk(-3))
-    to_twin(chunk(3))
-    arrived(out1)
-    out1 = [to(piece(-3).at[PART[0]], "z+"), to(piece(3).at[PART[1]], "z-")]
-    side += [(-3, to(piece(-3), "xs")), (3, to(piece(3), "xs"))]
+    next_one(0, 1)
+    next_one(1, 1)
+    settle(2)
+    next_one(0, 2)
+    next_one(1, 2)
+    settle(4)
     arrived(step)
     step = move(tz.at[3, 0], tz.at[4, 0], "z+")
-    arrived(out0)
-    to_twin(chunk(4))
-    arrived(out1)
-    side += [(4, to(piece(4), "xs"))]
-    for d, c in side:
-        c.wait_recv()
-        to_twin(ob.at[core, :, zat(d), 1])
+    next_one(0, 3)
+    next_one(1, 3)
+    settle(4)
+    for c in range(2):
+        arrived(out[c])
+        beside(c, 4)
+    settle(6)
     step.wait_recv()
     for s in range(3):
         v = tz[0, 0, s].astype(F32) + tz[4, 0, s].astype(F32)
         for k in (1, 2, 3):
             v = v + tz[k, 0, s].astype(F32) + tz[k, 1, s].astype(F32)
         t_ref[s] = v
+    done = [pltpu.make_async_copy(ob.at[core], o_ref.at[core], local.at[0])]
+    done[0].start()
     arrived(last)
-    done = pltpu.make_async_copy(ob, o_ref, local.at[0])
-    done.start()
-    done.wait()
+    done.append(pltpu.make_async_copy(ob.at[1 - core], o_ref.at[1 - core], local.at[1]))
+    done[1].start()
+    for c in done:
+        c.wait()
+    assert count[0] <= SEMAPHORES
     for c in sends:
         c.wait_send()
     for c in hops:
@@ -595,23 +643,22 @@
 
 
 def shards(features, labels, classifier, w_mix, w_point, kernels, counts):
-    tail = jnp.broadcast_to(counts[0].astype(BF), (3, 7, CH))
-    small = jnp.concatenate([kernels, tail], axis=1)
-
     lead = (16, CH)
     shape = lambda *d: pltpu.VMEM(d + lead, BF)
     maps = lambda n, t=BF: pltpu.VMEM((n, ROWS, CH), t)
-    n = 256
+    n = SEMAPHORES
     summed, taps = pl.pallas_call(
         kernel,
         out_shape=(jax.ShapeDtypeStruct((2, 3, 8, 2, 2, 16, CH), BF), jax.ShapeDtypeStruct((3, 16, CH), F32)),
         in_specs=[pl.BlockSpec(memory_space=pl.ANY)] * 4
-        + [pl.BlockSpec(memory_space=pltpu.VMEM), pl.BlockSpec(memory_space=pltpu.SMEM)],
+        + [pl.BlockSpec(memory_space=pltpu.VMEM)]
+        + [pl.BlockSpec(memory_space=pltpu.SMEM)] * 2,
         out_specs=(pl.BlockSpec(memory_space=pl.ANY), pl.BlockSpec(memory_space=pltpu.VMEM)),
         scratch_shapes=[
             pltpu.VMEM((2, CELLS, CH, CH), BF),
             pltpu.VMEM((CELLS, 16, CH), BF),
             pltpu.VMEM((GRID * GRID, CH), BF),
+            pltpu.VMEM((3, 9, CH), BF),
             maps(2),
             maps(2),
             pltpu.VMEM((2, GRID * GRID, CH), BF),
@@ -629,8 +676,8 @@
             shape(2, 3),
             shape(2, 3),
             shape(5, 2, 3),
-            shape(2, 2, 3, 2),
-            shape(2, 3, 2, 3, 2, 2),
+            shape(2, 2, 2, 3),
+            shape(2, 3, 2, 2, 3, 2),
             shape(2, 2, 3, 4),
             shape(2, 2, 3, 8),
             shape(2, 3),
@@ -643,9 +690,9 @@
             pltpu.SemaphoreType.DMA((n,)),
             pltpu.SemaphoreType.DMA((4,)),
         ],
-        compiler_params=pltpu.CompilerParams(collective_id=1, has_side_effects=True, vmem_limit_bytes=62 << 20),
+        compiler_params=pltpu.CompilerParams(collective_id=1, has_side_effects=True, vmem_limit_bytes=VMEM_MB << 20),
         name="step",
-    )(features, w_mix, w_point, small, classifier.T, labels)
+    )(features, w_mix, w_point, kernels, classifier.T, labels, counts)
     summed = summed.reshape(2, 3, CH, CH).astype(F32)
     return summed[0], summed[1], taps[:, :9]
 

time: 192 us -> 186 us (0.969)
  Pallas kernels: 182 us -> 176 us
    pallas_call x1, Pallas kernels: 182 us -> 176 us  [shards(): pl.pallas_call(kernel, out_shape=(jax.ShapeDtypeStruct((2, 3, 8, 2, 2, 16...]
where the time goes in v5:
time: 186 us; the launch traced here: 185 us
  Pallas kernels  176 us (95%)
  local copies, waits for them, and re-layouts  8.43 us (5%)
    pallas_call x1, Pallas kernels, shards(): pl.pallas_call(kernel, out_shape=(jax.ShapeDtypeStruct((2, 3, 8, 2, 2, 16...  176 us
    slice x1, local copies, waits for them, and re-layouts, shards(): return (summed[0], summed[1], taps[:, :9])  5.47 us

profile of v5, /device:TPU:1, one launch (start us, length us, event | category | flops | bytes accessed | tf_op | source)
XLA Modules:
  0.0 185.4 jit_solution(11874913718111249390)
XLA Ops:
  1.3 1.4 copy.10.tap_ref
  2.7 175.7 %step.1 = (bf16[2,3,8,2,2,16,512]{6,5,4,3,2,1,0:T(8,128)(2,1)}, f32[3,16,512]{2,1,0:T(8,128)}) custom-call(bf16[4,144,512]{2,1,0:T(8,128)(2,1)} %f_ref.1, bf16[3,512,512]{2,1,0:T(8,128)(2,1)} %mix_ref.1, bf16[3,512,512]{2,1,0:T(8,128)(2,1)} %point_ref.1, bf16[3,9,512]{2,1,0:T(8,128)(2,1)} %copy.10.tap_ref, f32[4,512]{1,0:T(4,128)} %bitcast.7, s32[4]{0:T(128)} %label_ref.1, ...), custom_call_target="tpu_custom_call" | custom-call | tf_op jit(solution)/shard_map/step/pallas_call | solution.py:650
  178.3 1.6 copy.11
  179.9 5.5 %fusion = (f32[1,3,8,2,2,16,512]{6,5,4,3,2,1,0:T(8,128)}, f32[1,3,8,2,2,16,512]{6,5,4,3,2,1,0:T(8,128)}) fusion(bf16[2,3,8,2,2,16,512]{6,5,4,3,2,1,0:T(8,128)(2,1)} %get-tuple-element.5), kind=kLoop, calls=%fused_computation | loop fusion | bytes 12582912 | tf_op jit(solution)/shard_map/slice | solution.py:697

commit v6 on v5

--- a/solution.py
+++ b/solution.py
@@ -640,6 +640,33 @@
         return 0
 
     lax.fori_loop(0, CELLS, sent, 0)
+
+
+def widen_kernel(x_ref, t_ref, mix_ref, point_ref, tap_ref):
+    mix_ref[...] = x_ref[0].astype(F32)
+    point_ref[...] = x_ref[1].astype(F32)
+
+    @pl.when(pl.program_id(0) == 0)
+    def _():
+        for s in range(3):
+            for tap in range(9):
+                tap_ref[tap, s : s + 1] = t_ref[s, tap : tap + 1]
+
+
+def widen(summed, taps):
+    out = pl.BlockSpec((1, CH, CH), lambda i: (i, 0, 0))
+    whole = jax.ShapeDtypeStruct((3, CH, CH), F32)
+    return pl.pallas_call(
+        widen_kernel,
+        grid=(3,),
+        in_specs=[
+            pl.BlockSpec((2, 1, CH, CH), lambda i: (0, i, 0, 0)),
+            pl.BlockSpec((3, 16, CH), lambda i: (0, 0, 0)),
+        ],
+        out_specs=[out, out, pl.BlockSpec((9, 3, CH), lambda i: (0, 0, 0))],
+        out_shape=[whole, whole, jax.ShapeDtypeStruct((9, 3, CH), F32)],
+        name="widen",
+    )(summed, taps)
 
 
 def shards(features, labels, classifier, w_mix, w_point, kernels, counts):
@@ -693,8 +720,8 @@
         compiler_params=pltpu.CompilerParams(collective_id=1, has_side_effects=True, vmem_limit_bytes=VMEM_MB << 20),
         name="step",
     )(features, w_mix, w_point, kernels, classifier.T, labels, counts)
-    summed = summed.reshape(2, 3, CH, CH).astype(F32)
-    return summed[0], summed[1], taps[:, :9]
+    mix, point, taps = widen(summed.reshape(2, 3, CH, CH), taps)
+    return mix, point, taps.transpose(1, 0, 2)
 
 
 def solution(mesh):

time: 186 us -> 184 us (0.989)
  local copies, waits for them, and re-layouts: 8.43 us -> 1.4 us
  Pallas kernels: 176 us -> 181 us
    slice x1 -> x0, local copies, waits for them, and re-layouts: 5.47 us -> none  [shards(): return (summed[0], summed[1], taps[:, :9])]
    pallas_call x0 -> x1, Pallas kernels: none -> 4.95 us  [widen(): pl.pallas_call(widen_kernel, grid=(3,), in_specs=[pl.BlockSpec((2, 1, CH,...]
where the time goes in v6:
time: 184 us; the launch traced here: 183 us
  Pallas kernels  181 us (98%)
    pallas_call x1, Pallas kernels, shards(): pl.pallas_call(kernel, out_shape=(jax.ShapeDtypeStruct((2, 3, 8, 2, 2, 16...  176 us
    pallas_call x1, Pallas kernels, widen(): pl.pallas_call(widen_kernel, grid=(3,), in_specs=[pl.BlockSpec((2, 1, CH,...  4.95 us

profile of v6, /device:TPU:1, one launch (start us, length us, event | category | flops | bytes accessed | tf_op | source)
XLA Modules:
  0.0 183.3 jit_solution(16354656861299347493)
XLA Ops:
  1.3 1.4 copy.10.tap_ref
  2.7 175.7 %step.1 = (bf16[2,3,8,2,2,16,512]{6,5,4,3,2,1,0:T(8,128)(2,1)}, f32[3,16,512]{2,1,0:T(8,128)}) custom-call(bf16[4,144,512]{2,1,0:T(8,128)(2,1)} %f_ref.1, bf16[3,512,512]{2,1,0:T(8,128)(2,1)} %mix_ref.1, bf16[3,512,512]{2,1,0:T(8,128)(2,1)} %point_ref.1, bf16[3,9,512]{2,1,0:T(8,128)(2,1)} %copy.10.tap_ref, f32[4,512]{1,0:T(4,128)} %bitcast.4, s32[4]{0:T(128)} %label_ref.1, ...), custom_call_target="tpu_custom_call" | custom-call | tf_op jit(solution)/shard_map/step/pallas_call | solution.py:677
  178.3 5.0 %widen.1 = (f32[3,512,512]{2,1,0:T(8,128)}, f32[3,512,512]{2,1,0:T(8,128)}, f32[9,3,512]{2,1,0:T(4,128)}) custom-call(bf16[2,3,512,512]{3,2,1,0:T(8,128)(2,1)} %bitcast.3, f32[3,16,512]{2,1,0:T(8,128)} %get-tuple-element.9.t_ref), custom_call_target="tpu_custom_call" | custom-call | tf_op jit(solution)/shard_map/widen/pallas_call | solution.py:659
